TPU v7x, 512 devices: a whole 4x4x16 slice. The times are simulated.
512 devices in a mesh: head: 4 (over y), seq: 16 (over z_lo, x), tp: 8 (over z_hi, core).
Axes of the slice: x: 4, y: 4, z: 16 (z_hi: 4, z_lo: 4; z = z_hi * 4 + z_lo), core: 2. Of those that a mesh axis runs over, the one named last changes fastest.
Arguments:
- queries: bfloat16 [4, 3072, 64, 128], P('head', 'seq', 'tp'), may hold values from -4.75 to 4.75
- keys: bfloat16 [3072, 8, 128], P(('seq', 'tp')), may hold values from -4.75 to 4.75
- values: bfloat16 [3072, 8, 128], P(('seq', 'tp')), may hold values from -4 to 4
- doc_ids: int32 [3072], P('seq'), may hold values from 0 to 3, never falling along the last dimension, each value on 1 to 1536 neighbouring positions
- output_gradient: bfloat16 [4, 3072, 64, 128], P('head', 'seq', 'tp'), may hold values from -6 to 6
- attention_output: bfloat16 [4, 3072, 64, 128], P('head', 'seq', 'tp'), may hold values from -4 to 4
Outputs:
- grad_queries: bfloat16 [4, 3072, 64, 128], P('head', 'seq', 'tp')
- grad_keys: bfloat16 [3072, 8, 128], P(('head', 'seq'), 'tp')
- grad_values: bfloat16 [3072, 8, 128], P(('head', 'seq'), 'tp')
Inputs may be any that keep to these rules, and one draw needn't show every extreme that they name: doc_ids never falls along the sequence; equal ids mark one packed document, the longest of 1536 positions.
All inputs are finite; a program needn't handle non-finite values.
Results may differ from a plain program's by a relative error of at most 0.006.
Values may be sent and summed in bfloat16 or wider, within the bound.
No kernel may reach another device: no remote copies, remote signals or barrier semaphores. Data moves between devices by JAX's collectives and lax.ppermute only.
A program may use at most 64 MiB of HBM per device.

v0:
```python
import jax
import jax.numpy as jnp
from jax import lax
from jax.sharding import PartitionSpec as P

NEG_FILL = -1e30


def on_device(queries, keys, values, doc_ids, output_gradient, attention_output):
    tokens = queries.shape[1]
    local_heads = queries.shape[2]
    head_dim = queries.shape[3]
    scale = head_dim ** (-0.5)
    key_local, value_local = (
        lax.all_to_all(keys, "tp", split_axis=1, concat_axis=0, tiled=True),
        lax.all_to_all(values, "tp", split_axis=1, concat_axis=0, tiled=True),
    )
    kv_groups = key_local.shape[1]
    query_group = local_heads // kv_groups
    all_keys, all_values, all_docs = (
        lax.all_gather(key_local, "seq", axis=0, tiled=True),
        lax.all_gather(value_local, "seq", axis=0, tiled=True),
        lax.all_gather(doc_ids, "seq", axis=0, tiled=True),
    )
    seq_total = all_keys.shape[0]
    seq_count = lax.axis_size("seq")
    per_block = min(seq_count, max(1, 512 // tokens))
    width = tokens * per_block
    blocks = seq_total // width
    query_grp = queries[0].reshape(tokens, kv_groups, query_group, head_dim)
    grad_grp = output_gradient[0].reshape(tokens, kv_groups, query_group, head_dim)
    out_grp = attention_output[0].reshape(tokens, kv_groups, query_group, head_dim)
    query_first = lax.axis_index("seq") * tokens
    query_last = query_first + tokens - 1
    query_pos = query_first + jnp.arange(tokens, dtype=jnp.int32)
    earliest = jnp.sum((all_docs < doc_ids[0]).astype(jnp.int32))
    key_pos = jnp.arange(seq_total, dtype=jnp.int32)
    block_starts = jnp.arange(blocks, dtype=jnp.int32) * width
    needed = (block_starts <= query_last) & (block_starts + width - 1 >= earliest)
    blocks_in = (
        all_keys.reshape(blocks, width, kv_groups, head_dim),
        all_values.reshape(blocks, width, kv_groups, head_dim),
        all_docs.reshape(blocks, width),
        key_pos.reshape(blocks, width),
        needed,
    )

    def scores_for(key_rows, doc_rows, pos_rows):
        score = (
            jnp.einsum("tcgd,jcd->cgtj", query_grp, key_rows, preferred_element_type=jnp.float32)
            * scale
        )
        allowed = (doc_rows[None, :] == doc_ids[:, None]) & (
            pos_rows[None, :] <= query_pos[:, None]
        )
        return (score, allowed[None, None])

    def stats_step(carry, block):
        key_rows, value_rows, doc_rows, pos_rows, used = block

        def stats_visit(state):
            top, total = state
            score, allowed = scores_for(key_rows, doc_rows, pos_rows)
            new_top = jnp.maximum(top, jnp.max(jnp.where(allowed, score, NEG_FILL), axis=3))
            weights = jnp.where(allowed, jnp.exp(score - new_top[..., None]), 0.0)
            total = total * jnp.exp(top - new_top) + jnp.sum(weights, axis=3)
            return (new_top, total)

        def stats_passing(state):
            return state

        return (lax.cond(used, stats_visit, stats_passing, carry), None)

    start_top = jnp.full((kv_groups, query_group, tokens), NEG_FILL, jnp.float32)
    start_total = jnp.zeros((kv_groups, query_group, tokens), jnp.float32)
    (top, total), unused = lax.scan(stats_step, (start_top, start_total), blocks_in)
    log_total = top + jnp.log(total)
    delta = jnp.transpose(
        jnp.sum(grad_grp.astype(jnp.float32) * out_grp.astype(jnp.float32), axis=3), (1, 2, 0)
    )
    zero_rows = jnp.zeros((kv_groups, query_group, tokens, head_dim), jnp.float32)

    def block_terms(key_rows, value_rows, doc_rows, pos_rows):
        score, allowed = scores_for(key_rows, doc_rows, pos_rows)
        prob = jnp.where(allowed, jnp.exp(score - log_total[..., None]), 0.0)
        prob_grad = jnp.einsum(
            "tcgd,jcd->cgtj", grad_grp, value_rows, preferred_element_type=jnp.float32
        )
        score_grad = (prob * (prob_grad - delta[..., None])).astype(jnp.bfloat16)
        return (prob.astype(jnp.bfloat16), score_grad)

    def key_value_terms(prob_low, score_grad):
        key_part = (
            jnp.einsum("cgtj,tcgd->jcd", score_grad, query_grp, preferred_element_type=jnp.float32)
            * scale
        )
        value_part = jnp.einsum(
            "cgtj,tcgd->jcd", prob_low, grad_grp, preferred_element_type=jnp.float32
        )
        return (key_part, value_part)

    share_rows = seq_total // (lax.axis_size("head") * seq_count)

    def grad_step(carry, block):
        key_rows, value_rows, doc_rows, pos_rows, used = block

        def grad_visit(accum):
            prob_low, score_grad = block_terms(key_rows, value_rows, doc_rows, pos_rows)
            accum = accum + jnp.einsum(
                "cgtj,jcd->cgtd", score_grad, key_rows, preferred_element_type=jnp.float32
            )
            key_part, value_part = key_value_terms(prob_low, score_grad)
            return (accum, key_part, value_part)

        def grad_passing(accum):
            empty = jnp.zeros((width, kv_groups, head_dim), jnp.float32)
            return (accum, empty, empty)

        accum, key_part, value_part = lax.cond(used, grad_visit, grad_passing, carry)
        return (accum, (key_part, value_part))

    query_accum, (key_parts, value_parts) = lax.scan(grad_step, zero_rows, blocks_in)
    key_full = key_parts.reshape(seq_total, kv_groups, head_dim)
    value_full = value_parts.reshape(seq_total, kv_groups, head_dim)
    head_count = lax.axis_size("head")

    def regroup(array):
        shaped = array.reshape(head_count, seq_count, share_rows, kv_groups, head_dim)
        return shaped.transpose(1, 0, 2, 3, 4).reshape(seq_total, kv_groups, head_dim)

    key_half, value_half = (
        lax.psum_scatter(regroup(key_full), "seq", scatter_dimension=0, tiled=True),
        lax.psum_scatter(regroup(value_full), "seq", scatter_dimension=0, tiled=True),
    )
    key_sum, value_sum = (
        lax.psum_scatter(key_half, "head", scatter_dimension=0, tiled=True),
        lax.psum_scatter(value_half, "head", scatter_dimension=0, tiled=True),
    )
    query_grad = jnp.transpose(query_accum * scale, (2, 0, 1, 3)).reshape(
        tokens, local_heads, head_dim
    )
    grad_queries = query_grad.astype(jnp.bfloat16)[None]
    return (grad_queries, key_sum.astype(jnp.bfloat16), value_sum.astype(jnp.bfloat16))


def solution(mesh):
    placed = (
        P("head", "seq", "tp", None),
        P(("seq", "tp"), None, None),
        P(("seq", "tp"), None, None),
        P("seq"),
        P("head", "seq", "tp", None),
        P("head", "seq", "tp", None),
    )
    return jax.shard_map(
        on_device,
        mesh=mesh,
        in_specs=placed,
        out_specs=(
            P("head", "seq", "tp", None),
            P(("head", "seq"), "tp", None),
            P(("head", "seq"), "tp", None),
        ),
        check_vma=False,
    )
```

profile of v0, /device:TPU:2, one launch (start us, length us, event | category | flops | bytes accessed | tf_op | source)
XLA Modules:
  0.0 509.1 jit_solution(2073579467774377939)
XLA Ops:
  7.2 1.4 copy.18
  8.6 15.1 %all-to-all-start.1 = ((bf16[24,8,128]{2,0,1:T(8,128)(2,1)}), bf16[24,8,128]{2,0,1:T(8,128)(2,1)S(1)}, u32[]{:S(2)}, u32[]{:S(2)}) async-start(bf16[24,8,128]{2,0,1:T(8,128)(2,1)} %copy.18), calls=%async_computation.1 | async-start | bytes 98304 | tf_op jit(solution)/shard_map/all_to_all | solution.py:16
  24.9 1.3 dynamic-slice
  27.7 72.6 %all-reduce = s32[3072]{0:T(1024)S(1)} all-reduce(s32[3072]{0:T(1024)S(1)} %dynamic-update-slice), channel_id=1, replica_groups=mesh['head'=4,'seq'=16,'tp'=8] {'seq'}, use_global_device_ids=true, to_apply=%add | all-reduce | flops 3072 | bytes 24576
  100.3 1.3 convert_reduce_fusion
  101.5 1.3 copy_bitcast_fusion
  103.9 1.4 copy.15
  105.4 2.1 fusion.51
  107.4 12.0 %all-to-all-start = ((bf16[24,8,128]{2,0,1:T(8,128)(2,1)}), bf16[24,8,128]{2,0,1:T(8,128)(2,1)S(1)}, u32[]{:S(2)}, u32[]{:S(2)}) async-start(bf16[24,8,128]{2,0,1:T(8,128)(2,1)} %copy.15), calls=%async_computation | async-start | bytes 98304 | tf_op jit(solution)/shard_map/all_to_all | solution.py:15
  119.5 47.3 %all_gather.11 = bf16[3072,1,128]{2,0,1:T(8,128)(2,1)S(1)} all-gather(bf16[192,1,128]{2,0,1:T(8,128)(2,1)S(1)} %bitcast.196), channel_id=1, replica_groups=mesh['head'=4,'seq'=16,'tp'=8] {'seq'}, dimensions={0}, use_global_device_ids=true | all-gather | bytes 835584 | tf_op jit(solution)/shard_map/all_gather | solution.py:22
  166.9 41.5 %all_gather.10 = bf16[3072,1,128]{2,0,1:T(8,128)(2,1)S(1)} all-gather(bf16[192,1,128]{2,0,1:T(8,128)(2,1)S(1)} %bitcast.197), channel_id=1, replica_groups=mesh['head'=4,'seq'=16,'tp'=8] {'seq'}, dimensions={0}, use_global_device_ids=true | all-gather | bytes 835584 | tf_op jit(solution)/shard_map/all_gather | solution.py:21
  208.3 16.0 %while.31 = (s32[]{:T(128)}, f32[1,8,192]{2,1,0:T(8,128)S(1)}, f32[1,8,192]{2,1,0:T(8,128)S(1)}, pred[8]{0:T(512)(128)(4,1)}, s32[8,384]{1,0:T(8,128)S(1)}, /*in...) while((s32[]{:T(128)}, f32[1,8,192]{2,1,0:T(8,128)S(1)}, ...), condition=%wide.region_6.7_spmd.clone, body=%wide.region_1.6_spmd.clone.sunk | while | flops 155348928 | bytes 5550596 | solution.py:76
  210.0 2.0 conditional.6
  225.0 24.3 %while.32 = (s32[]{:T(128)}, f32[1,8,192,128]{3,2,1,0:T(8,128)S(1)}, f32[8,384,1,128]{3,1,2,0:T(8,128)}, f32[8,384,1,128]{3,1,2,0:T(8,128)}, pred[8]{0:T(512)(12...) while((s32[]{:T(128)}, ...), condition=%wide.region_11.12_spmd.clone, body=%wide.region_8.11_spmd.clone.sunk | while | flops 761340864 | bytes 15570036 | solution.py:122
  226.7 3.9 conditional.7
  249.4 2.8 copy.25
  252.3 1.3 copy.24
  253.7 94.6 %reduce-scatter.9.cloned.1.call-done = f32[192,1,128]{2,0,1:T(8,128)} async-done(((f32[3072,1,128]{2,0,1:T(8,128)}), f32[192,1,128]{2,0,1:T(8,128)}) %reduce-scatter.9.cloned.1.call-update) | async-done | bytes 98320 | tf_op jit(solution)/shard_map/reduce_scatter | solution.py:133
  348.3 90.9 %reduce-scatter.5.cloned.1.call-done = f32[192,1,128]{2,0,1:T(8,128)} async-done(((f32[3072,1,128]{2,0,1:T(8,128)}), f32[192,1,128]{2,0,1:T(8,128)}) %reduce-scatter.5.cloned.1.call-update) | async-done | bytes 98320 | tf_op jit(solution)/shard_map/reduce_scatter | solution.py:132
  439.3 1.3 fusion.53
  440.5 30.0 %reduce-scatter.11.cloned.1.call-done = f32[48,1,128]{2,0,1:T(8,128)} async-done(((f32[192,1,128]{2,0,1:T(8,128)}), f32[48,1,128]{2,0,1:T(8,128)}) %reduce-scatter.11.cloned.1.call-update) | async-done | bytes 24592 | tf_op jit(solution)/shard_map/reduce_scatter | solution.py:137
  470.5 1.3 convert_element_type.80
  471.9 29.4 %reduce-scatter.7.cloned.1.call-done = f32[48,1,128]{2,0,1:T(8,128)} async-done(((f32[192,1,128]{2,0,1:T(8,128)}), f32[48,1,128]{2,0,1:T(8,128)}) %reduce-scatter.7.cloned.1.call-update) | async-done | bytes 24592 | tf_op jit(solution)/shard_map/reduce_scatter | solution.py:136
  501.3 1.3 convert_element_type.79
  (145 shorter events, 35.2 us)
Async XLA Ops:
  7.2 201.2 %copy-start.1 = (s32[192]{0:T(256)S(1)}, s32[192]{0:T(256)}, u32[]{:S(2)}) copy-start(s32[192]{0:T(256)} %param.17) | copy-start | bytes 2308
  8.6 98.8 %all-to-all-start.1 = ((bf16[24,8,128]{2,0,1:T(8,128)(2,1)}), bf16[24,8,128]{2,0,1:T(8,128)(2,1)S(1)}, u32[]{:S(2)}, u32[]{:S(2)}) async-start(bf16[24,8,128]{2,0,1:T(8,128)(2,1)} %copy.18), calls=%async_computation.1 | async-start | bytes 98304 | tf_op jit(solution)/shard_map/all_to_all | solution.py:16
  107.4 59.4 %all-to-all-start = ((bf16[24,8,128]{2,0,1:T(8,128)(2,1)}), bf16[24,8,128]{2,0,1:T(8,128)(2,1)S(1)}, u32[]{:S(2)}, u32[]{:S(2)}) async-start(bf16[24,8,128]{2,0,1:T(8,128)(2,1)} %copy.15), calls=%async_computation | async-start | bytes 98304 | tf_op jit(solution)/shard_map/all_to_all | solution.py:15
  119.5 228.8 %reduce-scatter.9.cloned.1.call-start = ((), (), s32[]{:S(2)}) async-start(), calls=%async_computation.8 | async-start | bytes 1671168 | tf_op jit(solution)/shard_map/reduce_scatter | solution.py:133
  226.8 0.7 copy-start.3
  227.5 1.0 copy-start.2
  249.3 2.9 copy-start
  252.2 187.0 %reduce-scatter.5.cloned.1.call-start = ((), (), s32[]{:S(2)}) async-start(), calls=%async_computation.6 | async-start | bytes 1671168 | tf_op jit(solution)/shard_map/reduce_scatter | solution.py:132
  253.6 216.9 %reduce-scatter.11.cloned.1.call-start = ((), (), s32[]{:S(2)}) async-start(), calls=%async_computation.9 | async-start | bytes 122880 | tf_op jit(solution)/shard_map/reduce_scatter | solution.py:137
  348.2 153.0 %reduce-scatter.7.cloned.1.call-start = ((), (), s32[]{:S(2)}) async-start(), calls=%async_computation.7 | async-start | bytes 122880 | tf_op jit(solution)/shard_map/reduce_scatter | solution.py:136
Sparse Core Ops, SparseCore 0:
  252.3 95.8 reduce-scatter.8
  351.3 87.9 reduce-scatter.4
  442.0 28.4 reduce-scatter.10
  473.4 27.8 reduce-scatter.6
where the time goes:
time: 510 us; the launch traced here: 509 us
  waiting for transfers between devices  245 us (48%)
  blocking collectives  161 us (32%)
  local copies, waits for them, and re-layouts  36.4 us (7%)
  starting transfers between devices  27.3 us (5%)
  between operations  14.5 us (3%)
  other arithmetic  10.4 us (2%)
  loops' own time  9.9 us (2%)
    reduce_scatter x1, waiting for transfers between devices, on_device(): lax.psum_scatter(regroup(value_full), 'seq', scatter_dimension=0, tiled=T...  94.6 us
    reduce_scatter x1, waiting for transfers between devices, on_device(): lax.psum_scatter(regroup(key_full), 'seq', scatter_dimension=0, tiled=True)  90.9 us
    unnamed x1, blocking collectives  72.6 us
    all_gather x1, blocking collectives, on_device(): lax.all_gather(value_local, 'seq', axis=0, tiled=True)  47.3 us
    all_gather x1, blocking collectives, on_device(): lax.all_gather(key_local, 'seq', axis=0, tiled=True)  41.5 us
    reduce_scatter x1, waiting for transfers between devices, on_device(): lax.psum_scatter(value_half, 'head', scatter_dimension=0, tiled=True)  30 us
    reduce_scatter x1, waiting for transfers between devices, on_device(): lax.psum_scatter(key_half, 'head', scatter_dimension=0, tiled=True)  29.4 us
    dynamic_slice x16, local copies, waits for them, and re-layouts, on_device(): lax.scan(stats_step, (start_top, start_total), blocks_in)  18.1 us
  transfers between devices with their start and end apart: 6, of which 4 were waited for; matrix products, arithmetic and copies ran while one was open for 3% of the time, Pallas kernels for 0%

commit v1 on v0

v1 whole, which is shorter than its diff:
```python
import functools
import jax
import jax.numpy as jnp
from jax import lax
from jax.experimental import pallas as pl
from jax.experimental.pallas import tpu as pltpu
from jax.sharding import PartitionSpec as P

F32, BF16 = jnp.float32, jnp.bfloat16
TOK = 192
BACK = 9
KB = 256
WIN = 1792
PAD = WIN - BACK * TOK
OWN = WIN - TOK
RT = 512
ROWS = 1536
HEADS = 8
LOG2E = 1.4426950408889634
NEG = -1e30
PAY = 208


def attention_kernel(
    where_ref, docs_ref, qdoc_ref, q_ref, do_ref, o_ref, own_ref, recv_ref,
    dq_ref, dkv_ref, kwin, vwin, dk_acc, dv_acc, t_scr,
):
    block = where_ref[0]
    x = lax.rem(block, 4)
    cnt = [jnp.zeros((1, 256), F32) for _ in range(3)]
    lane = lax.broadcasted_iota(jnp.int32, (1, 256), 1)
    kwin[0:PAD, :] = jnp.zeros((PAD, 128), BF16)
    vwin[0:PAD, :] = jnp.zeros((PAD, 128), BF16)
    for k in range(BACK):
        row = PAD + (BACK - 1 - k) * TOK
        if k % 4 == 0:
            src = own_ref.at[k // 4]
        else:
            src = recv_ref.at[lax.rem(x - k + 8, 4), k // 4]
        kwin[row:row + TOK, :] = src[0:TOK, 0:128]
        vwin[row:row + TOK, :] = src[0:TOK, 128:256]
        ids = src[TOK:TOK + 16, :].astype(F32)[0:1]
        ids = jnp.where(lane < TOK, ids, 100.0)
        for d in range(3):
            cnt[d] = cnt[d] + jnp.where(ids < d + 0.5, 1.0, 0.0)
    first_valid = OWN - block * TOK
    begin = [jnp.maximum(PAD, first_valid)]
    for d in range(3):
        begin.append(jnp.maximum(PAD + jnp.sum(cnt[d]).astype(jnp.int32), first_valid))

    def begin_of(doc):
        return jnp.where(
            doc == 0, begin[0], jnp.where(doc == 1, begin[1], jnp.where(doc == 2, begin[2], begin[3]))
        )

    dk_acc[...] = jnp.zeros_like(dk_acc)
    dv_acc[...] = jnp.zeros_like(dv_acc)
    c = (128.0 ** -0.5) * LOG2E
    tok_step = RT // HEADS
    last_kb = WIN // KB - 1

    def row_tile(i, unused):
        rows = pl.ds(pl.multiple_of(i * RT, RT), RT)
        q = q_ref[rows, :]
        do = do_ref[rows, :]
        delta = jnp.sum((do.astype(F32) * o_ref[rows, :].astype(F32)).T, axis=0, keepdims=True)
        start = begin_of(qdoc_ref[:, rows])
        tok = OWN + i * tok_step + lax.broadcasted_iota(jnp.int32, (1, RT), 1) // HEADS
        lo = begin_of(docs_ref[i * tok_step]) // KB
        mid = jnp.minimum((begin_of(docs_ref[i * tok_step + tok_step - 1]) + KB - 1) // KB, last_kb)

        def score_step(masked, kb, top):
            keys = pl.ds(pl.multiple_of(kb * KB, KB), KB)
            t = lax.dot_general(kwin[keys, :], q, (((1,), (1,)), ((), ())), preferred_element_type=F32) * c
            if masked:
                kp = kb * KB + lax.broadcasted_iota(jnp.int32, (KB, RT), 0)
                t = jnp.where((kp >= start) & (kp <= tok), t, NEG)
            t_scr[keys, :] = t
            return jnp.maximum(top, jnp.max(t.reshape(KB // 8, 8, RT), axis=0))

        top = jnp.full((8, RT), NEG, F32)
        top = lax.fori_loop(lo, mid, functools.partial(score_step, True), top)
        top = lax.fori_loop(mid, last_kb, functools.partial(score_step, False), top)
        top = score_step(True, last_kb, top)
        top = jnp.max(top, axis=0, keepdims=True)

        def exp_step(kb, total):
            keys = pl.ds(pl.multiple_of(kb * KB, KB), KB)
            e = jnp.exp2(t_scr[keys, :] - top)
            t_scr[keys, :] = e
            return total + jnp.sum(e.reshape(KB // 8, 8, RT), axis=0)

        total = lax.fori_loop(lo, last_kb + 1, exp_step, jnp.zeros((8, RT), F32))
        inv = 1.0 / jnp.sum(total, axis=0, keepdims=True)

        def grad_step(kb, dq):
            keys = pl.ds(pl.multiple_of(kb * KB, KB), KB)
            prob = t_scr[keys, :] * inv
            dp = lax.dot_general(vwin[keys, :], do, (((1,), (1,)), ((), ())), preferred_element_type=F32)
            ds = (prob * (dp - delta)).astype(BF16)
            dv_acc[keys, :] += jnp.dot(prob.astype(BF16), do, preferred_element_type=F32)
            dk_acc[keys, :] += jnp.dot(ds, q, preferred_element_type=F32)
            return dq + lax.dot_general(ds, kwin[keys, :], (((0,), (0,)), ((), ())), preferred_element_type=F32)

        dq = lax.fori_loop(lo, last_kb + 1, grad_step, jnp.zeros((RT, 128), F32))
        dq_ref[rows, :] = (dq * (128.0 ** -0.5)).astype(BF16)
        return unused

    lax.fori_loop(0, ROWS // RT, row_tile, 0)
    for k in range(BACK):
        row = PAD + (BACK - 1 - k) * TOK
        for r in range(4):
            part = slice(row + r * 48, row + r * 48 + 48)
            dkv_ref[r, k, :, 0:128] = dk_acc[part, :].astype(BF16)
            dkv_ref[r, k, :, 128:256] = dv_acc[part, :].astype(BF16)


def attention_grads(where, docs, qdoc, q, do, o, own, recv):
    vmem = pl.BlockSpec(memory_space=pltpu.VMEM)
    smem = pl.BlockSpec(memory_space=pltpu.SMEM)
    return pl.pallas_call(
        attention_kernel,
        out_shape=(
            jax.ShapeDtypeStruct((ROWS, 128), BF16),
            jax.ShapeDtypeStruct((4, BACK, 48, 256), BF16),
        ),
        in_specs=[smem, smem, vmem, vmem, vmem, vmem, vmem, vmem],
        out_specs=(vmem, vmem),
        scratch_shapes=[
            pltpu.VMEM((WIN, 128), BF16),
            pltpu.VMEM((WIN, 128), BF16),
            pltpu.VMEM((WIN, 128), F32),
            pltpu.VMEM((WIN, 128), F32),
            pltpu.VMEM((WIN, RT), F32),
        ],
        compiler_params=pltpu.CompilerParams(vmem_limit_bytes=40 << 20),
        cost_estimate=pl.CostEstimate(flops=3 << 30, bytes_accessed=3 << 20, transcendentals=2 << 20),
    )(where, docs, qdoc, q, do, o, own, recv)


X_GROUPS = [[4 * a + x for x in range(4)] for a in range(4)]


def on_device(queries, keys, values, doc_ids, output_gradient, attention_output):
    block = lax.axis_index("seq")
    a, x = block // 4, lax.rem(block, 4)
    kv = jnp.concatenate([keys, values], axis=2).transpose(1, 0, 2)
    kv = lax.all_to_all(kv, "tp", split_axis=0, concat_axis=0, tiled=True).reshape(TOK, 256)
    ids = jnp.pad(doc_ids.astype(BF16), (0, 64))
    tail = jnp.concatenate([ids[None], jnp.zeros((PAY - TOK - 1, 256), BF16)], axis=0)
    pay = jnp.concatenate([kv, tail], axis=0)
    back = [lax.ppermute(pay, "seq", [(i, i + k) for i in range(16 - k)]) for k in (4, 8)]
    own = jnp.stack([pay] + back)
    send = jnp.stack([jnp.where(x < dest, own[0:2], own[1:3]) for dest in range(4)])
    recv = lax.all_to_all(send, "seq", split_axis=0, concat_axis=0, tiled=True, axis_index_groups=X_GROUPS)
    qdoc = jnp.repeat(doc_ids, HEADS)[None]
    dq, dkv = attention_grads(
        block.reshape(1), doc_ids, qdoc,
        queries.reshape(ROWS, 128), output_gradient.reshape(ROWS, 128), attention_output.reshape(ROWS, 128),
        own, recv,
    )
    part = lax.all_to_all(dkv, "seq", split_axis=0, concat_axis=0, tiled=True, axis_index_groups=X_GROUPS)
    part = part.astype(F32)
    slots = []
    for j in range(12):
        terms = [part[xs, 8 + xs - j] for xs in range(4) if 0 <= 8 + xs - j < BACK]
        slots.append(sum(terms[1:], terms[0]))
    summed = jnp.stack(slots).astype(BF16).reshape(3, 4, 48, 256)
    wide = lax.dynamic_update_slice(jnp.zeros((6, 4, 48, 256), BF16), summed, (a, 0, 0, 0))[2:]
    wide = lax.all_to_all(wide, "head", split_axis=0, concat_axis=0, tiled=True)
    wide = jnp.sum(wide.astype(F32), axis=0).astype(BF16)
    z_groups = [[4 * i + j for i in range(4)] for j in range(4)]
    last = lax.all_to_all(wide, "seq", split_axis=0, concat_axis=0, tiled=True, axis_index_groups=z_groups)
    last = jnp.sum(last.astype(F32), axis=0)
    grad_keys = (last[:, 0:128] * (128.0 ** -0.5)).astype(BF16)[:, None]
    grad_values = last[:, 128:256].astype(BF16)[:, None]
    return dq.reshape(1, TOK, HEADS, 128), grad_keys, grad_values


def solution(mesh):
    placed = (
        P("head", "seq", "tp", None),
        P(("seq", "tp"), None, None),
        P(("seq", "tp"), None, None),
        P("seq"),
        P("head", "seq", "tp", None),
        P("head", "seq", "tp", None),
    )
    return jax.shard_map(
        on_device,
        mesh=mesh,
        in_specs=placed,
        out_specs=(
            P("head", "seq", "tp", None),
            P(("head", "seq"), "tp", None),
            P(("head", "seq"), "tp", None),
        ),
        check_vma=False,
    )
```

time: 510 us -> 113 us (0.22)
  the two profiles are of different devices: /device:TPU:2 before, /device:TPU:32 now
where the time goes in v1:
time: 113 us
  waiting for transfers between devices  39.2 us (35%)
  blocking collectives  31 us (27%)
  starting transfers between devices  29.4 us (26%)
  Pallas kernels  6.08 us (5%)
  other arithmetic  3.61 us (3%)
  local copies, waits for them, and re-layouts  2.63 us (2%)
    all_to_all x1, blocking collectives, on_device(): lax.all_to_all(wide, 'seq', split_axis=0, concat_axis=0, tiled=True, axis...  19.3 us
    all_to_all x1, waiting for transfers between devices, on_device(): lax.all_to_all(kv, 'tp', split_axis=0, concat_axis=0, tiled=True)  15.1 us
    all_to_all x1, starting transfers between devices, on_device(): lax.all_to_all(kv, 'tp', split_axis=0, concat_axis=0, tiled=True)  14.2 us
    all_to_all x1, blocking collectives, on_device(): wide = lax.all_to_all(wide, 'head', split_axis=0, concat_axis=0, tiled=True)  11.6 us
    all_to_all x1, waiting for transfers between devices, on_device(): lax.all_to_all(dkv, 'seq', split_axis=0, concat_axis=0, tiled=True, axis_...  10 us
    all_to_all x1, waiting for transfers between devices, on_device(): lax.all_to_all(send, 'seq', split_axis=0, concat_axis=0, tiled=True, axis...  9.59 us
    all_to_all x1, starting transfers between devices, on_device(): lax.all_to_all(dkv, 'seq', split_axis=0, concat_axis=0, tiled=True, axis_...  6.7 us
    pallas_call x1, Pallas kernels, attention_grads(): pl.pallas_call(attention_kernel, out_shape=(jax.ShapeDtypeStruct((ROWS, 1...  6.08 us
  transfers between devices with their start and end apart: 5, of which 5 were waited for; matrix products, arithmetic and copies ran while one was open for 1% of the time, Pallas kernels for 0%

profile of v1, /device:TPU:32, one launch (start us, length us, event | category | flops | bytes accessed | tf_op | source)
XLA Modules:
  0.0 112.8 jit_solution(18043561940322400962)
XLA Ops:
  0.6 0.8 copy.13
  1.4 0.8 copy.14
  2.2 0.7 maximum_bitcast_fusion
  2.9 14.2 %all-to-all-start = ((bf16[8,24,256]{2,1,0:T(8,128)(2,1)}), bf16[8,24,256]{2,1,0:T(8,128)(2,1)S(1)}, u32[]{:S(2)}, u32[]{:S(2)}) async-start(bf16[8,24,256]{2,1,0:T(8,128)(2,1)} %maximum_bitcast_fusion), calls=%async_computation | async-start | bytes 196608 | tf_op jit(solution)/shard_map/all_to_all | solution.py:148
  17.1 0.7 convert_element_type.22
  17.9 15.1 %all-to-all-done = bf16[8,24,256]{2,1,0:T(8,128)(2,1)S(1)} async-done(((bf16[8,24,256]{2,1,0:T(8,128)(2,1)}), bf16[8,24,256]{2,1,0:T(8,128)(2,1)S(1)}, u32[]{:S(2)}, u32[]{:S(2)}) %all-to-all-start) | async-done | bytes 98336 | tf_op jit(solution)/shard_map/all_to_all | solution.py:148
  33.0 0.1 fusion.23
  33.1 2.9 %collective-permute-start = (bf16[208,256]{1,0:T(8,128)(2,1)S(1)}, bf16[208,256]{1,0:T(8,128)(2,1)S(1)}, u32[]{:S(2)}, u32[]{:S(2)}) collective-permute-start(bf16[208,256]{1,0:T(8,128)(2,1)S(1)} %get-tuple-element.12), channel_id=1, source_target_pairs={{0,32},{8,40},{16,48},{24,56},{32,64},{40,72},{48,80},{56,88},{64,... | collective-permute-start | bytes 319496 | tf_op jit(solution)/shard_map/ppermute | solution.py:152
  36.0 1.3 %collective-permute-start.1 = (bf16[208,256]{1,0:T(8,128)(2,1)S(1)}, bf16[208,256]{1,0:T(8,128)(2,1)S(1)}, u32[]{:S(2)}, u32[]{:S(2)}) collective-permute-start(bf16[208,256]{1,0:T(8,128)(2,1)S(1)} %get-tuple-element.12), channel_id=1, source_target_pairs={{0,64},{8,72},{16,80},{24,88},{32,96},{40,104},{48,112},{56,120},{... | collective-permute-start | bytes 319496 | tf_op jit(solution)/shard_map/ppermute | solution.py:152
  37.3 3.4 %collective-permute-done = bf16[208,256]{1,0:T(8,128)(2,1)S(1)} collective-permute-done((bf16[208,256]{1,0:T(8,128)(2,1)S(1)}, bf16[208,256]{1,0:T(8,128)(2,1)S(1)}, u32[]{:S(2)}, u32[]{:S(2)}) %collective-permute-start) | collective-permute-done | bytes 106528 | tf_op jit(solution)/shard_map/ppermute | solution.py:152
  40.7 1.1 collective-permute-done.1
  42.0 1.0 pad_maximum_fusion
  43.0 4.3 %all-to-all-start.1 = ((bf16[4,2,208,256]{3,2,1,0:T(8,128)(2,1)}), bf16[4,2,208,256]{3,2,1,0:T(8,128)(2,1)S(1)}, u32[]{:S(2)}, u32[]{:S(2)}) async-start(bf16[4,2,208,256]{3,2,1,0:T(8,128)(2,1)} %pad_maximum_fusion), calls=%async_computation.1 | async-start | bytes 1703936 | tf_op jit(solution)/shard_map/all_to_all | solution.py:155
  47.3 0.1 broadcast_in_dim.18
  47.4 0.1 broadcast_in_dim_reshape.3.qdoc_ref
  47.5 9.6 %all-to-all-done.1.recv_ref = bf16[4,2,208,256]{3,2,1,0:T(8,128)(2,1)S(1)} async-done(((bf16[4,2,208,256]{3,2,1,0:T(8,128)(2,1)}), bf16[4,2,208,256]{3,2,1,0:T(8,128)(2,1)S(1)}, u32[]{:S(2)}, u32[]{:S(2)}) %all-to-all-start.1) | async-done | bytes 852000 | tf_op jit(solution)/shard_map/all_to_all | solution.py:155
  57.1 6.1 %shard_map.85 = (bf16[1536,128]{1,0:T(8,128)(2,1)}, bf16[4,9,48,256]{3,2,1,0:T(8,128)(2,1)}) custom-call(s32[1]{0:T(128)} %bitcast.where_ref, s32[192]{0:T(256)S(1)} %copy-done, s32[1,1536]{1,0:T(1,128)S(1)} %broadcast_in_dim_reshape.3.qdoc_ref, bf16[1536,128]{1,0:T(8,128)(2,1)S(1)} %bitcast.69, bf16[1536,128]{1,0:T(8,128)(2,1)S(1)} %bitcast.70, ...), custom_call_target="tpu_custom_call" | custom-call | flops 3221225472 | bytes 3145728 | tf_op jit(solution)/shard_map/pallas_call | solution.py:121
  63.2 6.7 %all-to-all-start.2 = ((bf16[4,9,48,256]{3,2,1,0:T(8,128)(2,1)}), bf16[4,9,48,256]{3,2,1,0:T(8,128)(2,1)S(1)}, u32[]{:S(2)}, u32[]{:S(2)}) async-start(bf16[4,9,48,256]{3,2,1,0:T(8,128)(2,1)} %get-tuple-element.6), calls=%async_computation.2 | async-start | bytes 1769472 | tf_op jit(solution)/shard_map/all_to_all | solution.py:162
  69.9 10.0 %all-to-all-done.2 = bf16[4,9,48,256]{3,2,1,0:T(8,128)(2,1)S(1)} async-done(((bf16[4,9,48,256]{3,2,1,0:T(8,128)(2,1)}), bf16[4,9,48,256]{3,2,1,0:T(8,128)(2,1)S(1)}, u32[]{:S(2)}, u32[]{:S(2)}) %all-to-all-start.2) | async-done | bytes 884768 | tf_op jit(solution)/shard_map/all_to_all | solution.py:162
  79.9 0.2 convert_element_type.23
  80.5 11.6 %all_to_all.25 = bf16[4,4,48,256]{3,2,1,0:T(8,128)(2,1)S(1)} all-to-all(bf16[4,4,48,256]{3,2,1,0:T(8,128)(2,1)S(1)} %slice.205), channel_id=1, replica_groups=mesh['head'=4,'seq'=16,'tp'=8] {'head'}, dimensions={0} | all-to-all | bytes 786432 | tf_op jit(solution)/shard_map/all_to_all | solution.py:170
  92.2 19.3 %all_to_all.26 = bf16[4,48,256]{2,1,0:T(8,128)(2,1)S(1)} all-to-all(bf16[4,48,256]{2,1,0:T(8,128)(2,1)S(1)} %reduce_sum.21), channel_id=1, replica_groups={{0,32,64,96},{8,40,72,104},{16,48,80,112},{24,56,88,120},{1,33,65,97},{..., dimensions={0} | all-to-all | bytes 196608 | tf_op jit(solution)/shard_map/all_to_all | solution.py:173
  111.5 0.6 fusion.21
  112.2 0.6 fusion.22
  (32 shorter events, 0.6 us)
Async XLA Ops:
  2.9 30.1 %all-to-all-start = ((bf16[8,24,256]{2,1,0:T(8,128)(2,1)}), bf16[8,24,256]{2,1,0:T(8,128)(2,1)S(1)}, u32[]{:S(2)}, u32[]{:S(2)}) async-start(bf16[8,24,256]{2,1,0:T(8,128)(2,1)} %maximum_bitcast_fusion), calls=%async_computation | async-start | bytes 196608 | tf_op jit(solution)/shard_map/all_to_all | solution.py:148
  33.1 7.6 %collective-permute-start = (bf16[208,256]{1,0:T(8,128)(2,1)S(1)}, bf16[208,256]{1,0:T(8,128)(2,1)S(1)}, u32[]{:S(2)}, u32[]{:S(2)}) collective-permute-start(bf16[208,256]{1,0:T(8,128)(2,1)S(1)} %get-tuple-element.12), channel_id=1, source_target_pairs={{0,32},{8,40},{16,48},{24,56},{32,64},{40,72},{48,80},{56,88},{64,... | collective-permute-start | bytes 319496 | tf_op jit(solution)/shard_map/ppermute | solution.py:152
  36.0 5.8 %collective-permute-start.1 = (bf16[208,256]{1,0:T(8,128)(2,1)S(1)}, bf16[208,256]{1,0:T(8,128)(2,1)S(1)}, u32[]{:S(2)}, u32[]{:S(2)}) collective-permute-start(bf16[208,256]{1,0:T(8,128)(2,1)S(1)} %get-tuple-element.12), channel_id=1, source_target_pairs={{0,64},{8,72},{16,80},{24,88},{32,96},{40,104},{48,112},{56,120},{... | collective-permute-start | bytes 319496 | tf_op jit(solution)/shard_map/ppermute | solution.py:152
  41.9 5.4 %copy-start = (s32[192]{0:T(256)S(1)}, s32[192]{0:T(256)}, u32[]{:S(2)}) copy-start(s32[192]{0:T(256)} %docs_ref.1) | copy-start | bytes 2308
  41.9 15.2 %copy-start.1 = (bf16[1,192,8,128]{3,2,1,0:T(8,128)(2,1)S(1)}, bf16[1,192,8,128]{3,2,1,0:T(8,128)(2,1)}, u32[]{:S(2)}) copy-start(bf16[1,192,8,128]{3,2,1,0:T(8,128)(2,1)} %param.6) | copy-start | bytes 1179652
  41.9 15.2 %copy-start.2 = (bf16[1,192,8,128]{3,2,1,0:T(8,128)(2,1)S(1)}, bf16[1,192,8,128]{3,2,1,0:T(8,128)(2,1)}, u32[]{:S(2)}) copy-start(bf16[1,192,8,128]{3,2,1,0:T(8,128)(2,1)} %param.10) | copy-start | bytes 1179652
  42.0 15.2 %copy-start.3 = (bf16[1,192,8,128]{3,2,1,0:T(8,128)(2,1)S(1)}, bf16[1,192,8,128]{3,2,1,0:T(8,128)(2,1)}, u32[]{:S(2)}) copy-start(bf16[1,192,8,128]{3,2,1,0:T(8,128)(2,1)} %param.11) | copy-start | bytes 1179652
  43.0 14.1 %all-to-all-start.1 = ((bf16[4,2,208,256]{3,2,1,0:T(8,128)(2,1)}), bf16[4,2,208,256]{3,2,1,0:T(8,128)(2,1)S(1)}, u32[]{:S(2)}, u32[]{:S(2)}) async-start(bf16[4,2,208,256]{3,2,1,0:T(8,128)(2,1)} %pad_maximum_fusion), calls=%async_computation.1 | async-start | bytes 1703936 | tf_op jit(solution)/shard_map/all_to_all | solution.py:155
  63.2 16.7 %all-to-all-start.2 = ((bf16[4,9,48,256]{3,2,1,0:T(8,128)(2,1)}), bf16[4,9,48,256]{3,2,1,0:T(8,128)(2,1)S(1)}, u32[]{:S(2)}, u32[]{:S(2)}) async-start(bf16[4,9,48,256]{3,2,1,0:T(8,128)(2,1)} %get-tuple-element.6), calls=%async_computation.2 | async-start | bytes 1769472 | tf_op jit(solution)/shard_map/all_to_all | solution.py:162

commit v2 on v1

v2 whole, which is shorter than its diff:
```python
import functools
import jax
import jax.numpy as jnp
from jax import lax
from jax.experimental import pallas as pl
from jax.experimental.pallas import tpu as pltpu
from jax.sharding import PartitionSpec as P

F32, BF16 = jnp.float32, jnp.bfloat16
TOK = 192
BACK = 9
KB = 576
LAST = BACK * TOK // KB - 1
ROWS = 1536
HEADS = 8
LOG2E = 1.4426950408889634
NEG = -1e30
SCALE2 = (128.0 ** -0.5) * LOG2E
OWN = (BACK - 1) * TOK
PAY = 208
NT = (((1,), (1,)), ((), ()))
TN = (((0,), (0,)), ((), ()))


def keys_of(k):
    return pl.ds(pl.multiple_of(k * KB, KB), KB)


def load_window(where_ref, own_ref, recv_ref, kwin, vwin):
    block = where_ref[0]
    x = lax.rem(block, 4)
    cnt = [jnp.zeros((1, 256), F32) for _ in range(3)]
    lane = lax.broadcasted_iota(jnp.int32, (1, 256), 1)
    for k in range(BACK):
        if k % 4 == 0:
            src = own_ref.at[k // 4]
        else:
            src = recv_ref.at[lax.rem(x - k + 8, 4), k // 4]
        place = slice((BACK - 1 - k) * TOK, (BACK - k) * TOK)
        kwin[place, :] = src[0:TOK, 0:128]
        vwin[place, :] = src[0:TOK, 128:256]
        ids = src[TOK:TOK + 16, :].astype(F32)[0:1]
        ids = jnp.where(lane < TOK, ids, 100.0)
        for d in range(3):
            cnt[d] = cnt[d] + jnp.where(ids < d + 0.5, 1.0, 0.0)
    first_valid = jnp.maximum(OWN - block * TOK, 0)
    begin = [first_valid]
    for d in range(3):
        begin.append(jnp.maximum(jnp.sum(cnt[d]).astype(jnp.int32), first_valid))
    return begin


def begin_of(begin, doc):
    return jnp.where(
        doc == 0, begin[0], jnp.where(doc == 1, begin[1], jnp.where(doc == 2, begin[2], begin[3]))
    )


def scaled_scores(key, q, start, k, masked, own):
    t = lax.dot_general(key, q, NT, preferred_element_type=F32) * SCALE2
    if masked or own:
        kp = lax.broadcasted_iota(jnp.int32, (KB, ROWS), 0)
        allowed = kp >= start - k * KB
        if own:
            tok = OWN - LAST * KB + lax.broadcasted_iota(jnp.int32, (1, ROWS), 1) // HEADS
            allowed = allowed & (kp <= tok)
        t = jnp.where(allowed, t, NEG)
    return t


def over_window(step, low, mid):
    lax.fori_loop(low, mid, functools.partial(step, masked=True, own=False), 0)
    lax.fori_loop(mid, LAST, functools.partial(step, masked=False, own=False), 0)
    step(LAST, 0, True, True)


def key_value_kernel(
    where_ref, docs_ref, qdoc_ref, q_ref, do_ref, o_ref, own_ref, recv_ref,
    dkv_ref, stat_ref, kwin, vwin, t_scr, m_scr, l_scr, start_scr,
):
    begin = load_window(where_ref, own_ref, recv_ref, kwin, vwin)
    start_scr[...] = begin_of(begin, qdoc_ref[...])
    low = begin_of(begin, docs_ref[0]) // KB
    mid = jnp.minimum((begin_of(begin, docs_ref[TOK - 1]) + KB - 1) // KB, LAST)
    m_scr[...] = jnp.full_like(m_scr, NEG)
    l_scr[...] = jnp.zeros_like(l_scr)

    def score_step(k, unused, masked, own):
        t = scaled_scores(kwin[keys_of(k), :], q_ref[...], start_scr[...], k, masked, own)
        t_scr[keys_of(k), :] = t
        t = t.reshape(KB // 8, 8, ROWS)
        old = m_scr[...]
        top = jnp.maximum(old, jnp.max(t, axis=0))
        m_scr[...] = top
        l_scr[...] = l_scr[...] * jnp.exp2(old - top) + jnp.sum(jnp.exp2(t - top), axis=0)
        return unused

    over_window(score_step, low, mid)
    top = jnp.max(m_scr[...], axis=0, keepdims=True)
    total = jnp.sum(l_scr[...] * jnp.exp2(m_scr[...] - top), axis=0, keepdims=True)
    stat_ref[0:1, :] = top + jnp.log(total) * LOG2E
    stat_ref[1:2, :] = jnp.sum((do_ref[...].astype(F32) * o_ref[...].astype(F32)).T, axis=0, keepdims=True)

    def grad_step(k, unused):
        q, do = q_ref[...], do_ref[...]
        prob = jnp.exp2(t_scr[keys_of(k), :] - stat_ref[0:1, :])
        dp = lax.dot_general(vwin[keys_of(k), :], do, NT, preferred_element_type=F32)
        ds = (prob * (dp - stat_ref[1:2, :])).astype(BF16)
        dv = jnp.dot(prob.astype(BF16), do, preferred_element_type=F32)
        dk = jnp.dot(ds, q, preferred_element_type=F32)
        for b in range(KB // TOK):
            for r in range(4):
                part = slice(b * TOK + r * 48, b * TOK + r * 48 + 48)
                back = BACK - 1 - b - k * (KB // TOK)
                dkv_ref[r, back, :, 0:128] = dk[part].astype(BF16)
                dkv_ref[r, back, :, 128:256] = dv[part].astype(BF16)
        return unused

    lax.fori_loop(low, LAST + 1, grad_step, 0)

    def clear_step(k, unused):
        for b in range(KB // TOK):
            for r in range(4):
                dkv_ref[r, BACK - 1 - b - k * (KB // TOK)] = jnp.zeros((48, 256), BF16)
        return unused

    lax.fori_loop(0, low, clear_step, 0)


def query_kernel(
    where_ref, docs_ref, qdoc_ref, q_ref, do_ref, stat_ref, own_ref, recv_ref,
    dq_ref, kwin, vwin, dq_acc, start_scr,
):
    begin = load_window(where_ref, own_ref, recv_ref, kwin, vwin)
    start_scr[...] = begin_of(begin, qdoc_ref[...])
    low = begin_of(begin, docs_ref[0]) // KB
    mid = jnp.minimum((begin_of(begin, docs_ref[TOK - 1]) + KB - 1) // KB, LAST)
    dq_acc[...] = jnp.zeros_like(dq_acc)

    def query_step(k, unused, masked, own):
        key = kwin[keys_of(k), :]
        t = scaled_scores(key, q_ref[...], start_scr[...], k, masked, own)
        prob = jnp.exp2(t - stat_ref[0:1, :])
        dp = lax.dot_general(vwin[keys_of(k), :], do_ref[...], NT, preferred_element_type=F32)
        ds = (prob * (dp - stat_ref[1:2, :])).astype(BF16)
        dq_acc[...] += lax.dot_general(key, ds, TN, preferred_element_type=F32)
        return unused

    over_window(query_step, low, mid)
    dq_ref[...] = (dq_acc[...].T * (128.0 ** -0.5)).astype(BF16)


VMEM_SPEC = pl.BlockSpec(memory_space=pltpu.VMEM)
SMEM_SPEC = pl.BlockSpec(memory_space=pltpu.SMEM)


def key_value_grads(where, docs, qdoc, q, do, o, own, recv):
    return pl.pallas_call(
        key_value_kernel,
        out_shape=(
            jax.ShapeDtypeStruct((4, BACK, 48, 256), BF16),
            jax.ShapeDtypeStruct((8, ROWS), F32),
        ),
        in_specs=[SMEM_SPEC, SMEM_SPEC] + [VMEM_SPEC] * 6,
        out_specs=(VMEM_SPEC, VMEM_SPEC),
        scratch_shapes=[
            pltpu.VMEM((BACK * TOK, 128), BF16),
            pltpu.VMEM((BACK * TOK, 128), BF16),
            pltpu.VMEM((BACK * TOK, ROWS), F32),
            pltpu.VMEM((8, ROWS), F32),
            pltpu.VMEM((8, ROWS), F32),
            pltpu.VMEM((1, ROWS), jnp.int32),
        ],
        compiler_params=pltpu.CompilerParams(vmem_limit_bytes=40 << 20),
        cost_estimate=pl.CostEstimate(flops=4 << 30, bytes_accessed=3 << 20, transcendentals=2 << 20),
    )(where, docs, qdoc, q, do, o, own, recv)


def query_grads(where, docs, qdoc, q, do, stat, own, recv):
    return pl.pallas_call(
        query_kernel,
        out_shape=jax.ShapeDtypeStruct((ROWS, 128), BF16),
        in_specs=[SMEM_SPEC, SMEM_SPEC] + [VMEM_SPEC] * 6,
        out_specs=VMEM_SPEC,
        scratch_shapes=[
            pltpu.VMEM((BACK * TOK, 128), BF16),
            pltpu.VMEM((BACK * TOK, 128), BF16),
            pltpu.VMEM((128, ROWS), F32),
            pltpu.VMEM((1, ROWS), jnp.int32),
        ],
        compiler_params=pltpu.CompilerParams(vmem_limit_bytes=40 << 20),
        cost_estimate=pl.CostEstimate(flops=3 << 30, bytes_accessed=3 << 20, transcendentals=2 << 20),
    )(where, docs, qdoc, q, do, stat, own, recv)


def attention_grads(where, docs, qdoc, q, do, o, own, recv):
    dkv, stat = key_value_grads(where, docs, qdoc, q, do, o, own, recv)
    return query_grads(where, docs, qdoc, q, do, stat, own, recv), dkv


X_GROUPS = [[4 * a + x for x in range(4)] for a in range(4)]


def on_device(queries, keys, values, doc_ids, output_gradient, attention_output):
    block = lax.axis_index("seq")
    a, x = block // 4, lax.rem(block, 4)
    kv = jnp.concatenate([keys, values], axis=2).transpose(1, 0, 2)
    kv = lax.all_to_all(kv, "tp", split_axis=0, concat_axis=0, tiled=True).reshape(TOK, 256)
    ids = jnp.pad(doc_ids.astype(BF16), (0, 64))
    tail = jnp.concatenate([ids[None], jnp.zeros((PAY - TOK - 1, 256), BF16)], axis=0)
    pay = jnp.concatenate([kv, tail], axis=0)
    back = [lax.ppermute(pay, "seq", [(i, i + k) for i in range(16 - k)]) for k in (4, 8)]
    own = jnp.stack([pay] + back)
    send = jnp.stack([jnp.where(x < dest, own[0:2], own[1:3]) for dest in range(4)])
    recv = lax.all_to_all(send, "seq", split_axis=0, concat_axis=0, tiled=True, axis_index_groups=X_GROUPS)
    qdoc = jnp.repeat(doc_ids, HEADS)[None]
    dq, dkv = attention_grads(
        block.reshape(1), doc_ids, qdoc,
        queries.reshape(ROWS, 128), output_gradient.reshape(ROWS, 128), attention_output.reshape(ROWS, 128),
        own, recv,
    )
    part = lax.all_to_all(dkv, "seq", split_axis=0, concat_axis=0, tiled=True, axis_index_groups=X_GROUPS)
    part, dq = lax.optimization_barrier((part, dq))
    part = part.astype(F32)
    slots = []
    for j in range(12):
        terms = [part[xs, 8 + xs - j] for xs in range(4) if 0 <= 8 + xs - j < BACK]
        slots.append(sum(terms[1:], terms[0]))
    summed = jnp.stack(slots).astype(BF16).reshape(3, 4, 48, 256)
    wide = lax.dynamic_update_slice(jnp.zeros((6, 4, 48, 256), BF16), summed, (a, 0, 0, 0))[2:]
    last = lax.all_to_all(
        wide.reshape(16, 48, 256), ("head", "seq"), split_axis=0, concat_axis=0, tiled=True,
        axis_index_groups=[[16 * h + 4 * z + xs for h in range(4) for z in range(4)] for xs in range(4)],
    )
    last = jnp.sum(last.astype(F32), axis=0)
    grad_keys = (last[:, 0:128] * (128.0 ** -0.5)).astype(BF16)[:, None]
    grad_values = last[:, 128:256].astype(BF16)[:, None]
    return dq.reshape(1, TOK, HEADS, 128), grad_keys, grad_values


def solution(mesh):
    placed = (
        P("head", "seq", "tp", None),
        P(("seq", "tp"), None, None),
        P(("seq", "tp"), None, None),
        P("seq"),
        P("head", "seq", "tp", None),
        P("head", "seq", "tp", None),
    )
    return jax.shard_map(
        on_device,
        mesh=mesh,
        in_specs=placed,
        out_specs=(
            P("head", "seq", "tp", None),
            P(("head", "seq"), "tp", None),
            P(("head", "seq"), "tp", None),
        ),
        check_vma=False,
    )
```

time: 113 us -> 99.2 us (0.88)
  the two profiles are of different devices: /device:TPU:32 before, /device:TPU:2 now
where the time goes in v2:
time: 99.2 us; the launch traced here: 98.7 us
  starting transfers between devices  33.7 us (34%)
  waiting for transfers between devices  32.2 us (32%)
  blocking collectives  17.6 us (18%)
  Pallas kernels  8.07 us (8%)
  other arithmetic  3.59 us (4%)
  local copies, waits for them, and re-layouts  2.63 us (3%)
    all_to_all x1, blocking collectives, on_device(): lax.all_to_all(wide.reshape(16, 48, 256), ('head', 'seq'), split_axis=0,...  17.6 us
    all_to_all x1, starting transfers between devices, on_device(): lax.all_to_all(kv, 'tp', split_axis=0, concat_axis=0, tiled=True)  15.1 us
    all_to_all x1, waiting for transfers between devices, on_device(): lax.all_to_all(kv, 'tp', split_axis=0, concat_axis=0, tiled=True)  13.4 us
    all_to_all x1, waiting for transfers between devices, on_device(): lax.all_to_all(send, 'seq', split_axis=0, concat_axis=0, tiled=True, axis...  10.3 us
    ppermute x2, starting transfers between devices, on_device(): lax.ppermute(pay, 'seq', [(i, i + k) for i in range(16 - k)])  7 us
    all_to_all x1, starting transfers between devices, on_device(): lax.all_to_all(dkv, 'seq', split_axis=0, concat_axis=0, tiled=True, axis_...  6.81 us
    all_to_all x1, waiting for transfers between devices, on_device(): lax.all_to_all(dkv, 'seq', split_axis=0, concat_axis=0, tiled=True, axis_...  6.15 us
    all_to_all x1, starting transfers between devices, on_device(): lax.all_to_all(send, 'seq', split_axis=0, concat_axis=0, tiled=True, axis...  4.82 us
  transfers between devices with their start and end apart: 5, of which 5 were waited for; matrix products, arithmetic and copies ran while one was open for 1% of the time, Pallas kernels for 3%

profile of v2, /device:TPU:2, one launch (start us, length us, event | category | flops | bytes accessed | tf_op | source)
XLA Modules:
  0.0 98.7 jit_solution(14922881302281437032)
XLA Ops:
  0.6 0.8 copy.11
  1.4 0.8 copy.12
  2.2 0.7 maximum_bitcast_fusion
  2.9 15.1 %all-to-all-start = ((bf16[8,24,256]{2,1,0:T(8,128)(2,1)}), bf16[8,24,256]{2,1,0:T(8,128)(2,1)S(1)}, u32[]{:S(2)}, u32[]{:S(2)}) async-start(bf16[8,24,256]{2,1,0:T(8,128)(2,1)} %maximum_bitcast_fusion), calls=%async_computation | async-start | bytes 196608 | tf_op jit(solution)/shard_map/all_to_all | solution.py:208
  18.0 0.7 convert_element_type.20
  18.8 13.4 %all-to-all-done = bf16[8,24,256]{2,1,0:T(8,128)(2,1)S(1)} async-done(((bf16[8,24,256]{2,1,0:T(8,128)(2,1)}), bf16[8,24,256]{2,1,0:T(8,128)(2,1)S(1)}, u32[]{:S(2)}, u32[]{:S(2)}) %all-to-all-start) | async-done | bytes 98336 | tf_op jit(solution)/shard_map/all_to_all | solution.py:208
  32.2 0.1 fusion.23
  32.3 4.6 %collective-permute-start = (bf16[208,256]{1,0:T(8,128)(2,1)S(1)}, bf16[208,256]{1,0:T(8,128)(2,1)S(1)}, u32[]{:S(2)}, u32[]{:S(2)}) collective-permute-start(bf16[208,256]{1,0:T(8,128)(2,1)S(1)} %get-tuple-element.16), channel_id=1, source_target_pairs={{0,32},{8,40},{16,48},{24,56},{32,64},{40,72},{48,80},{56,88},{64,... | collective-permute-start | bytes 319496 | tf_op jit(solution)/shard_map/ppermute | solution.py:212
  36.9 2.4 %collective-permute-start.1 = (bf16[208,256]{1,0:T(8,128)(2,1)S(1)}, bf16[208,256]{1,0:T(8,128)(2,1)S(1)}, u32[]{:S(2)}, u32[]{:S(2)}) collective-permute-start(bf16[208,256]{1,0:T(8,128)(2,1)S(1)} %get-tuple-element.16), channel_id=1, source_target_pairs={{0,64},{8,72},{16,80},{24,88},{32,96},{40,104},{48,112},{56,120},{... | collective-permute-start | bytes 319496 | tf_op jit(solution)/shard_map/ppermute | solution.py:212
  39.3 0.8 collective-permute-done
  40.2 1.4 %collective-permute-done.1 = bf16[208,256]{1,0:T(8,128)(2,1)S(1)} collective-permute-done((bf16[208,256]{1,0:T(8,128)(2,1)S(1)}, bf16[208,256]{1,0:T(8,128)(2,1)S(1)}, u32[]{:S(2)}, u32[]{:S(2)}) %collective-permute-start.1) | collective-permute-done | bytes 106528 | tf_op jit(solution)/shard_map/ppermute | solution.py:212
  41.7 1.0 %pad_maximum_fusion = bf16[4,2,208,256]{3,2,1,0:T(8,128)(2,1)} fusion(bf16[1,2,208,256]{3,2,1,0:T(8,128)(2,1)S(1)} %broadcast_select_fusion, bf16[1,2,208,256]{3,2,1,0:T(8,128)(2,1)S(1)} %get-tuple-element.13, bf16[1,2,208,256]{3,2,1,0:T(8,128)(2,1)S(1)} %get-tuple-element.12, bf16[1,2,208,256]{3,2,1,0:T(8,128)(2,1)S(1)} %get-tuple-element.11), kind=kLoop, calls=%fused_computation | loop fusion | flops 1277952 | bytes 1703936 | tf_op jit(solution)/shard_map/stack | solution.py:214
  42.7 4.8 %all-to-all-start.1 = ((bf16[4,2,208,256]{3,2,1,0:T(8,128)(2,1)}), bf16[4,2,208,256]{3,2,1,0:T(8,128)(2,1)S(1)}, u32[]{:S(2)}, u32[]{:S(2)}) async-start(bf16[4,2,208,256]{3,2,1,0:T(8,128)(2,1)} %pad_maximum_fusion), calls=%async_computation.1 | async-start | bytes 1703936 | tf_op jit(solution)/shard_map/all_to_all | solution.py:215
  47.6 0.1 broadcast_in_dim.18
  47.6 0.1 broadcast_in_dim_reshape.3.qdoc_ref
  47.8 10.3 %all-to-all-done.1.recv_ref = bf16[4,2,208,256]{3,2,1,0:T(8,128)(2,1)S(1)} async-done(((bf16[4,2,208,256]{3,2,1,0:T(8,128)(2,1)}), bf16[4,2,208,256]{3,2,1,0:T(8,128)(2,1)S(1)}, u32[]{:S(2)}, u32[]{:S(2)}) %all-to-all-start.1) | async-done | bytes 852000 | tf_op jit(solution)/shard_map/all_to_all | solution.py:215
  58.2 4.8 %shard_map.85 = (bf16[4,9,48,256]{3,2,1,0:T(8,128)(2,1)}, f32[8,1536]{1,0:T(8,128)S(1)}) custom-call(s32[1]{0:T(128)} %bitcast.where_ref, s32[192]{0:T(256)S(1)} %copy-done, s32[1,1536]{1,0:T(1,128)S(1)} %broadcast_in_dim_reshape.3.qdoc_ref, bf16[1536,128]{1,0:T(8,128)(2,1)S(1)} %bitcast.67, bf16[1536,128]{1,0:T(8,128)(2,1)S(1)} %bitcast.69, ...), custom_call_target="tpu_custom_call" | custom-call | flops 4294967296 | bytes 3145728 | tf_op jit(solution)/shard_map/pallas_call | solution.py:158
  62.9 6.8 %all-to-all-start.2 = ((bf16[4,9,48,256]{3,2,1,0:T(8,128)(2,1)}), bf16[4,9,48,256]{3,2,1,0:T(8,128)(2,1)S(1)}, u32[]{:S(2)}, u32[]{:S(2)}) async-start(bf16[4,9,48,256]{3,2,1,0:T(8,128)(2,1)} %get-tuple-element.7), calls=%async_computation.2 | async-start | bytes 1769472 | tf_op jit(solution)/shard_map/all_to_all | solution.py:222
  69.7 3.3 %shard_map.86 = bf16[1536,128]{1,0:T(8,128)(2,1)} custom-call(s32[1]{0:T(128)} %bitcast.where_ref, s32[192]{0:T(256)S(1)} %copy-done, s32[1,1536]{1,0:T(1,128)S(1)} %broadcast_in_dim_reshape.3.qdoc_ref, bf16[1536,128]{1,0:T(8,128)(2,1)S(1)} %bitcast.68, bf16[1536,128]{1,0:T(8,128)(2,1)S(1)} %bitcast.70, f32[8,1536]{1,0:T(8,128)S(1)} %get-tuple-element.8.stat_ref, ...), custom_call_target="tpu_custom_call" | custom-call | flops 3221225472 | bytes 3145728 | tf_op jit(solution)/shard_map/pallas_call | solution.py:180
  73.0 6.2 %all-to-all-done.2 = bf16[4,9,48,256]{3,2,1,0:T(8,128)(2,1)S(1)} async-done(((bf16[4,9,48,256]{3,2,1,0:T(8,128)(2,1)}), bf16[4,9,48,256]{3,2,1,0:T(8,128)(2,1)S(1)}, u32[]{:S(2)}, u32[]{:S(2)}) %all-to-all-start.2) | async-done | bytes 884768 | tf_op jit(solution)/shard_map/all_to_all | solution.py:222
  79.2 0.2 convert_element_type.21
  79.8 17.6 %all_to_all.20 = bf16[16,48,256]{2,1,0:T(8,128)(2,1)S(1)} all-to-all(bf16[16,48,256]{2,1,0:T(8,128)(2,1)S(1)} %bitcast.71), channel_id=1, replica_groups={{0,32,64,96,128,160,192,224,256,288,320,352,384,416,448,480},{8,40,72,1..., dimensions={0} | all-to-all | bytes 786432 | tf_op jit(solution)/shard_map/all_to_all | solution.py:231
  97.5 0.6 fusion.21
  98.1 0.6 fusion.22
  (31 shorter events, 0.5 us)
Async XLA Ops:
  2.9 29.3 %all-to-all-start = ((bf16[8,24,256]{2,1,0:T(8,128)(2,1)}), bf16[8,24,256]{2,1,0:T(8,128)(2,1)S(1)}, u32[]{:S(2)}, u32[]{:S(2)}) async-start(bf16[8,24,256]{2,1,0:T(8,128)(2,1)} %maximum_bitcast_fusion), calls=%async_computation | async-start | bytes 196608 | tf_op jit(solution)/shard_map/all_to_all | solution.py:208
  32.3 7.9 %collective-permute-start = (bf16[208,256]{1,0:T(8,128)(2,1)S(1)}, bf16[208,256]{1,0:T(8,128)(2,1)S(1)}, u32[]{:S(2)}, u32[]{:S(2)}) collective-permute-start(bf16[208,256]{1,0:T(8,128)(2,1)S(1)} %get-tuple-element.16), channel_id=1, source_target_pairs={{0,32},{8,40},{16,48},{24,56},{32,64},{40,72},{48,80},{56,88},{64,... | collective-permute-start | bytes 319496 | tf_op jit(solution)/shard_map/ppermute | solution.py:212
  36.9 4.7 %collective-permute-start.1 = (bf16[208,256]{1,0:T(8,128)(2,1)S(1)}, bf16[208,256]{1,0:T(8,128)(2,1)S(1)}, u32[]{:S(2)}, u32[]{:S(2)}) collective-permute-start(bf16[208,256]{1,0:T(8,128)(2,1)S(1)} %get-tuple-element.16), channel_id=1, source_target_pairs={{0,64},{8,72},{16,80},{24,88},{32,96},{40,104},{48,112},{56,120},{... | collective-permute-start | bytes 319496 | tf_op jit(solution)/shard_map/ppermute | solution.py:212
  41.7 5.9 %copy-start = (s32[192]{0:T(256)S(1)}, s32[192]{0:T(256)}, u32[]{:S(2)}) copy-start(s32[192]{0:T(256)} %docs_ref.3) | copy-start | bytes 2308
  41.7 16.5 %copy-start.1 = (bf16[1,192,8,128]{3,2,1,0:T(8,128)(2,1)S(1)}, bf16[1,192,8,128]{3,2,1,0:T(8,128)(2,1)}, u32[]{:S(2)}) copy-start(bf16[1,192,8,128]{3,2,1,0:T(8,128)(2,1)} %param.11) | copy-start | bytes 1179652
  41.7 16.5 %copy-start.2 = (bf16[1,192,8,128]{3,2,1,0:T(8,128)(2,1)S(1)}, bf16[1,192,8,128]{3,2,1,0:T(8,128)(2,1)}, u32[]{:S(2)}) copy-start(bf16[1,192,8,128]{3,2,1,0:T(8,128)(2,1)} %param.6) | copy-start | bytes 1179652
  41.7 16.5 %copy-start.3 = (bf16[1,192,8,128]{3,2,1,0:T(8,128)(2,1)S(1)}, bf16[1,192,8,128]{3,2,1,0:T(8,128)(2,1)}, u32[]{:S(2)}) copy-start(bf16[1,192,8,128]{3,2,1,0:T(8,128)(2,1)} %param.10) | copy-start | bytes 1179652
  42.7 15.4 %all-to-all-start.1 = ((bf16[4,2,208,256]{3,2,1,0:T(8,128)(2,1)}), bf16[4,2,208,256]{3,2,1,0:T(8,128)(2,1)S(1)}, u32[]{:S(2)}, u32[]{:S(2)}) async-start(bf16[4,2,208,256]{3,2,1,0:T(8,128)(2,1)} %pad_maximum_fusion), calls=%async_computation.1 | async-start | bytes 1703936 | tf_op jit(solution)/shard_map/all_to_all | solution.py:215
  62.9 16.3 %all-to-all-start.2 = ((bf16[4,9,48,256]{3,2,1,0:T(8,128)(2,1)}), bf16[4,9,48,256]{3,2,1,0:T(8,128)(2,1)S(1)}, u32[]{:S(2)}, u32[]{:S(2)}) async-start(bf16[4,9,48,256]{3,2,1,0:T(8,128)(2,1)} %get-tuple-element.7), calls=%async_computation.2 | async-start | bytes 1769472 | tf_op jit(solution)/shard_map/all_to_all | solution.py:222

commit v3 on v2

--- a/solution.py
+++ b/solution.py
@@ -17,7 +17,7 @@
 NEG = -1e30
 SCALE2 = (128.0 ** -0.5) * LOG2E
 OWN = (BACK - 1) * TOK
-PAY = 208
+PAY = 200
 NT = (((1,), (1,)), ((), ()))
 TN = (((0,), (0,)), ((), ()))
 
@@ -39,7 +39,7 @@
         place = slice((BACK - 1 - k) * TOK, (BACK - k) * TOK)
         kwin[place, :] = src[0:TOK, 0:128]
         vwin[place, :] = src[0:TOK, 128:256]
-        ids = src[TOK:TOK + 16, :].astype(F32)[0:1]
+        ids = src[TOK:TOK + 8, :].astype(F32)[0:1]
         ids = jnp.where(lane < TOK, ids, 100.0)
         for d in range(3):
             cnt[d] = cnt[d] + jnp.where(ids < d + 0.5, 1.0, 0.0)
@@ -198,14 +198,79 @@
     return query_grads(where, docs, qdoc, q, do, stat, own, recv), dkv
 
 
+def sum_kernel(group_ref, part_ref, out_ref):
+    first = 4 * group_ref[0] - 8
+    out_ref[...] = jnp.zeros_like(out_ref)
+    for j in range(12):
+
+        @pl.when(first + j >= 0)
+        def _():
+            terms = [part_ref[xs, 8 + xs - j].astype(F32) for xs in range(4) if 0 <= 8 + xs - j < BACK]
+            out_ref[jnp.maximum(first + j, 0)] = sum(terms[1:], terms[0]).astype(BF16)
+
+
+def sum_terms(group, part):
+    return pl.pallas_call(
+        sum_kernel,
+        out_shape=jax.ShapeDtypeStruct((16, 48, 256), BF16),
+        in_specs=[SMEM_SPEC, VMEM_SPEC],
+        out_specs=VMEM_SPEC,
+        compiler_params=pltpu.CompilerParams(vmem_limit_bytes=8 << 20),
+        cost_estimate=pl.CostEstimate(flops=1 << 20, bytes_accessed=1 << 20, transcendentals=0),
+    )(group, part)
+
+
+def finish_kernel(last_ref, dk_ref, dv_ref):
+    total = jnp.sum(last_ref[...].astype(F32), axis=0)
+    dk_ref[...] = (total[:, 0:128] * (128.0 ** -0.5)).astype(BF16)
+    dv_ref[...] = total[:, 128:256].astype(BF16)
+
+
+def finish(last):
+    return pl.pallas_call(
+        finish_kernel,
+        out_shape=(jax.ShapeDtypeStruct((48, 128), BF16),) * 2,
+        in_specs=[VMEM_SPEC],
+        out_specs=(VMEM_SPEC, VMEM_SPEC),
+        compiler_params=pltpu.CompilerParams(vmem_limit_bytes=8 << 20),
+        cost_estimate=pl.CostEstimate(flops=1 << 18, bytes_accessed=1 << 19, transcendentals=0),
+    )(last)
+
+
 X_GROUPS = [[4 * a + x for x in range(4)] for a in range(4)]
 
 
 def on_device(queries, keys, values, doc_ids, output_gradient, attention_output):
     block = lax.axis_index("seq")
     a, x = block // 4, lax.rem(block, 4)
-    kv = jnp.concatenate([keys, values], axis=2).transpose(1, 0, 2)
-    kv = lax.all_to_all(kv, "tp", split_axis=0, concat_axis=0, tiled=True).reshape(TOK, 256)
+    tp = lax.axis_index("tp")
+    core, half = tp % 2 == 1, tp >= 4
+    near = ((tp // 2) % 2 == 1) != half
+    bits = (half, near, core)
+
+    def by_label(array):
+        for axis, bit in enumerate(bits):
+            array = jnp.where(bit, jnp.flip(array, axis), array)
+        return array
+
+    def relabel(array):
+        return jnp.stack([array[0:2], jnp.flip(array[2:4], 0)])
+
+    def by_core(array):
+        return jnp.where(core, jnp.swapaxes(array, 0, 1), array)
+
+    def swap(array, flip0, flip1):
+        return lax.ppermute(array, "tp", [(i, i ^ (flip1 if i % 2 else flip0)) for i in range(8)])
+
+    kv = jnp.concatenate([keys, values], axis=2).transpose(1, 0, 2).reshape(4, 2, 24, 256)
+    part = by_label(relabel(kv))
+    got = swap(part[:, :, 1], 1, 1)
+    part = by_core(jnp.stack([part[:, :, 0], got], axis=2))
+    got = swap(part[:, 1], 2, 6)
+    part = jnp.stack([part[:, 0], got], axis=1)
+    got = swap(part[1], 6, 2)
+    part = by_label(by_core(jnp.stack([part[0], got])))
+    kv = jnp.concatenate([part[0], jnp.flip(part[1], 0)]).reshape(TOK, 256)
     ids = jnp.pad(doc_ids.astype(BF16), (0, 64))
     tail = jnp.concatenate([ids[None], jnp.zeros((PAY - TOK - 1, 256), BF16)], axis=0)
     pay = jnp.concatenate([kv, tail], axis=0)
@@ -221,20 +286,12 @@
     )
     part = lax.all_to_all(dkv, "seq", split_axis=0, concat_axis=0, tiled=True, axis_index_groups=X_GROUPS)
     part, dq = lax.optimization_barrier((part, dq))
-    part = part.astype(F32)
-    slots = []
-    for j in range(12):
-        terms = [part[xs, 8 + xs - j] for xs in range(4) if 0 <= 8 + xs - j < BACK]
-        slots.append(sum(terms[1:], terms[0]))
-    summed = jnp.stack(slots).astype(BF16).reshape(3, 4, 48, 256)
-    wide = lax.dynamic_update_slice(jnp.zeros((6, 4, 48, 256), BF16), summed, (a, 0, 0, 0))[2:]
     last = lax.all_to_all(
-        wide.reshape(16, 48, 256), ("head", "seq"), split_axis=0, concat_axis=0, tiled=True,
+        sum_terms(a.reshape(1), part), ("head", "seq"), split_axis=0, concat_axis=0, tiled=True,
         axis_index_groups=[[16 * h + 4 * z + xs for h in range(4) for z in range(4)] for xs in range(4)],
     )
-    last = jnp.sum(last.astype(F32), axis=0)
-    grad_keys = (last[:, 0:128] * (128.0 ** -0.5)).astype(BF16)[:, None]
-    grad_values = last[:, 128:256].astype(BF16)[:, None]
+    grad_keys, grad_values = finish(last)
+    grad_keys, grad_values = grad_keys[:, None], grad_values[:, None]
     return dq.reshape(1, TOK, HEADS, 128), grad_keys, grad_values
 
 

time: 99.2 us -> 98.5 us (level)
  the two profiles are of different devices: /device:TPU:2 before, /device:TPU:128 now
where the time goes in v3:
time: 98.5 us; the launch traced here: 97.9 us
  starting transfers between devices  33.4 us (34%)
  blocking collectives  25.7 us (26%)
  waiting for transfers between devices  25.5 us (26%)
  Pallas kernels  8.89 us (9%)
  other arithmetic  2.2 us (2%)
  local copies, waits for them, and re-layouts  1.22 us (1%)
  between operations  1.01 us (1%)
    all_to_all x1, blocking collectives, on_device(): lax.all_to_all(sum_terms(a.reshape(1), part), ('head', 'seq'), split_axis...  25.7 us
    ppermute x3, starting transfers between devices, swap(): lax.ppermute(array, 'tp', [(i, i ^ (flip1 if i % 2 else flip0)) for i in...  17 us
    all_to_all x1, waiting for transfers between devices, on_device(): lax.all_to_all(send, 'seq', split_axis=0, concat_axis=0, tiled=True, axis...  9.71 us
    ppermute x2, starting transfers between devices, on_device(): lax.ppermute(pay, 'seq', [(i, i + k) for i in range(16 - k)])  8.42 us
    ppermute x3, waiting for transfers between devices, swap(): lax.ppermute(array, 'tp', [(i, i ^ (flip1 if i % 2 else flip0)) for i in...  6.98 us
    all_to_all x1, waiting for transfers between devices, on_device(): lax.all_to_all(dkv, 'seq', split_axis=0, concat_axis=0, tiled=True, axis_...  6.64 us
    pallas_call x1, Pallas kernels, key_value_grads(): pl.pallas_call(key_value_kernel, out_shape=(jax.ShapeDtypeStruct((4, BACK...  4.8 us
    all_to_all x1, starting transfers between devices, on_device(): lax.all_to_all(send, 'seq', split_axis=0, concat_axis=0, tiled=True, axis...  4.42 us
  transfers between devices with their start and end apart: 7, of which 6 were waited for; matrix products, arithmetic and copies ran while one was open for 0% of the time, Pallas kernels for 3%

profile of v3, /device:TPU:128, one launch (start us, length us, event | category | flops | bytes accessed | tf_op | source)
XLA Modules:
  0.0 97.9 jit_solution(12513593121470981169)
XLA Ops:
  0.7 0.7 copy-done.4
  1.4 0.8 maximum_bitcast_fusion
  2.5 1.9 %collective-permute-start = (bf16[2,2,24,256]{3,2,0,1:T(8,128)(2,1)S(1)}, bf16[2,2,24,256]{3,2,0,1:T(8,128)(2,1)S(1)}, u32[]{:S(2)}, u32[]{:S(2)}) collective-permute-start(bf16[2,2,24,256]{3,2,0,1:T(8,128)(2,1)S(1)} %get-tuple-element.28), channel_id=1, source_target_pairs={{0,1},{1,0},{2,3},{3,2},{4,5},{5,4},{6,7},{7,6},{8,9},{9,8},{10,11... | collective-permute-start | bytes 147464 | tf_op jit(solution)/shard_map/ppermute | solution.py:263
  4.5 1.2 %collective-permute-done = bf16[2,2,24,256]{3,2,0,1:T(8,128)(2,1)S(1)} collective-permute-done((bf16[2,2,24,256]{3,2,0,1:T(8,128)(2,1)S(1)}, bf16[2,2,24,256]{3,2,0,1:T(8,128)(2,1)S(1)}, u32[]{:S(2)}, u32[]{:S(2)}) %collective-permute-start) | collective-permute-done | bytes 49184 | tf_op jit(solution)/shard_map/ppermute | solution.py:263
  5.7 6.0 %collective-permute-start.1 = (bf16[2,2,24,256]{3,2,1,0:T(8,128)(2,1)S(1)}, bf16[2,2,24,256]{3,2,1,0:T(8,128)(2,1)S(1)}, u32[]{:S(2)}, u32[]{:S(2)}) collective-permute-start(bf16[2,2,24,256]{3,2,1,0:T(8,128)(2,1)S(1)} %get-tuple-element.26), channel_id=1, source_target_pairs={{0,2},{1,7},{2,0},{3,5},{4,6},{5,3},{6,4},{7,1},{8,10},{9,15},{10,... | collective-permute-start | bytes 147464 | tf_op jit(solution)/shard_map/ppermute | solution.py:263
  11.7 3.9 %collective-permute-done.1 = bf16[2,2,24,256]{3,2,1,0:T(8,128)(2,1)S(1)} collective-permute-done((bf16[2,2,24,256]{3,2,1,0:T(8,128)(2,1)S(1)}, bf16[2,2,24,256]{3,2,1,0:T(8,128)(2,1)S(1)}, u32[]{:S(2)}, u32[]{:S(2)}) %collective-permute-start.1) | collective-permute-done | bytes 49184 | tf_op jit(solution)/shard_map/ppermute | solution.py:263
  15.6 9.1 %collective-permute-start.2 = (bf16[2,2,24,256]{3,2,1,0:T(8,128)(2,1)S(1)}, bf16[2,2,24,256]{3,2,1,0:T(8,128)(2,1)S(1)}, u32[]{:S(2)}, u32[]{:S(2)}) collective-permute-start(bf16[2,2,24,256]{3,2,1,0:T(8,128)(2,1)S(1)} %get-tuple-element.24), channel_id=1, source_target_pairs={{0,6},{1,3},{2,4},{3,1},{4,2},{5,7},{6,0},{7,5},{8,14},{9,11},{10,... | collective-permute-start | bytes 147464 | tf_op jit(solution)/shard_map/ppermute | solution.py:263
  24.9 1.9 %collective-permute-done.2 = bf16[2,2,24,256]{3,2,1,0:T(8,128)(2,1)S(1)} collective-permute-done((bf16[2,2,24,256]{3,2,1,0:T(8,128)(2,1)S(1)}, bf16[2,2,24,256]{3,2,1,0:T(8,128)(2,1)S(1)}, u32[]{:S(2)}, u32[]{:S(2)}) %collective-permute-start.2) | collective-permute-done | bytes 49184 | tf_op jit(solution)/shard_map/ppermute | solution.py:263
  26.9 0.1 fusion.4
  27.0 3.0 %collective-permute-start.3 = (bf16[200,256]{1,0:T(8,128)(2,1)S(1)}, bf16[200,256]{1,0:T(8,128)(2,1)S(1)}, u32[]{:S(2)}, u32[]{:S(2)}) collective-permute-start(bf16[200,256]{1,0:T(8,128)(2,1)S(1)} %get-tuple-element.20), channel_id=1, source_target_pairs={{0,32},{8,40},{16,48},{24,56},{32,64},{40,72},{48,80},{56,88},{64,... | collective-permute-start | bytes 307208 | tf_op jit(solution)/shard_map/ppermute | solution.py:277
  30.0 5.4 %collective-permute-start.4 = (bf16[200,256]{1,0:T(8,128)(2,1)S(1)}, bf16[200,256]{1,0:T(8,128)(2,1)S(1)}, u32[]{:S(2)}, u32[]{:S(2)}) collective-permute-start(bf16[200,256]{1,0:T(8,128)(2,1)S(1)} %get-tuple-element.20), channel_id=1, source_target_pairs={{0,64},{8,72},{16,80},{24,88},{32,96},{40,104},{48,112},{56,120},{... | collective-permute-start | bytes 307208 | tf_op jit(solution)/shard_map/ppermute | solution.py:277
  35.5 2.2 %collective-permute-done.4 = bf16[200,256]{1,0:T(8,128)(2,1)S(1)} collective-permute-done((bf16[200,256]{1,0:T(8,128)(2,1)S(1)}, bf16[200,256]{1,0:T(8,128)(2,1)S(1)}, u32[]{:S(2)}, u32[]{:S(2)}) %collective-permute-start.4) | collective-permute-done | bytes 102432 | tf_op jit(solution)/shard_map/ppermute | solution.py:277
  37.8 1.0 %pad_maximum_fusion = bf16[4,2,200,256]{3,2,1,0:T(8,128)(2,1)} fusion(bf16[1,2,200,256]{3,2,1,0:T(8,128)(2,1)S(1)} %broadcast_select_fusion, bf16[1,2,200,256]{3,2,1,0:T(8,128)(2,1)S(1)} %get-tuple-element.17, bf16[1,2,200,256]{3,2,1,0:T(8,128)(2,1)S(1)} %get-tuple-element.16, bf16[1,2,200,256]{3,2,1,0:T(8,128)(2,1)S(1)} %get-tuple-element.15), kind=kLoop, calls=%fused_computation | loop fusion | flops 1228800 | bytes 1638400 | tf_op jit(solution)/shard_map/stack | solution.py:279
  38.8 4.4 %all-to-all-start = ((bf16[4,2,200,256]{3,2,1,0:T(8,128)(2,1)}), bf16[4,2,200,256]{3,2,1,0:T(8,128)(2,1)S(1)}, u32[]{:S(2)}, u32[]{:S(2)}) async-start(bf16[4,2,200,256]{3,2,1,0:T(8,128)(2,1)} %pad_maximum_fusion), calls=%async_computation | async-start | bytes 1638400 | tf_op jit(solution)/shard_map/all_to_all | solution.py:280
  43.2 0.1 broadcast_in_dim.15
  43.3 0.1 broadcast_in_dim_reshape.3.qdoc_ref
  43.5 9.7 %all-to-all-done.recv_ref = bf16[4,2,200,256]{3,2,1,0:T(8,128)(2,1)S(1)} async-done(((bf16[4,2,200,256]{3,2,1,0:T(8,128)(2,1)}), bf16[4,2,200,256]{3,2,1,0:T(8,128)(2,1)S(1)}, u32[]{:S(2)}, u32[]{:S(2)}) %all-to-all-start) | async-done | bytes 819232 | tf_op jit(solution)/shard_map/all_to_all | solution.py:280
  53.2 4.8 %shard_map.85 = (bf16[4,9,48,256]{3,2,1,0:T(8,128)(2,1)}, f32[8,1536]{1,0:T(8,128)S(1)}) custom-call(s32[1]{0:T(128)} %bitcast.where_ref, s32[192]{0:T(256)S(1)} %copy-done, s32[1,1536]{1,0:T(1,128)S(1)} %broadcast_in_dim_reshape.3.qdoc_ref, bf16[1536,128]{1,0:T(8,128)(2,1)S(1)} %bitcast.49, bf16[1536,128]{1,0:T(8,128)(2,1)S(1)} %bitcast.51, ...), custom_call_target="tpu_custom_call" | custom-call | flops 4294967296 | bytes 3145728 | tf_op jit(solution)/shard_map/pallas_call | solution.py:158
  58.0 3.5 %all-to-all-start.1 = ((bf16[4,9,48,256]{3,2,1,0:T(8,128)(2,1)}), bf16[4,9,48,256]{3,2,1,0:T(8,128)(2,1)S(1)}, u32[]{:S(2)}, u32[]{:S(2)}) async-start(bf16[4,9,48,256]{3,2,1,0:T(8,128)(2,1)} %get-tuple-element.9), calls=%async_computation.1 | async-start | bytes 1769472 | tf_op jit(solution)/shard_map/all_to_all | solution.py:287
  61.5 3.3 %shard_map.86 = bf16[1536,128]{1,0:T(8,128)(2,1)} custom-call(s32[1]{0:T(128)} %bitcast.where_ref, s32[192]{0:T(256)S(1)} %copy-done, s32[1,1536]{1,0:T(1,128)S(1)} %broadcast_in_dim_reshape.3.qdoc_ref, bf16[1536,128]{1,0:T(8,128)(2,1)S(1)} %bitcast.50, bf16[1536,128]{1,0:T(8,128)(2,1)S(1)} %bitcast.52, f32[8,1536]{1,0:T(8,128)S(1)} %get-tuple-element.10.stat_ref, ...), custom_call_target="tpu_custom_call" | custom-call | flops 3221225472 | bytes 3145728 | tf_op jit(solution)/shard_map/pallas_call | solution.py:180
  64.8 6.6 %all-to-all-done.1.part_ref = bf16[4,9,48,256]{3,2,1,0:T(8,128)(2,1)S(1)} async-done(((bf16[4,9,48,256]{3,2,1,0:T(8,128)(2,1)}), bf16[4,9,48,256]{3,2,1,0:T(8,128)(2,1)S(1)}, u32[]{:S(2)}, u32[]{:S(2)}) %all-to-all-start.1) | async-done | bytes 884768 | tf_op jit(solution)/shard_map/all_to_all | solution.py:287
  71.5 0.1 shard_map.87
  71.6 25.7 %all_to_all.15.last_ref = bf16[16,48,256]{2,1,0:T(8,128)(2,1)S(1)} all-to-all(bf16[16,48,256]{2,1,0:T(8,128)(2,1)S(1)} %shard_map.87), channel_id=1, replica_groups={{0,32,64,96,128,160,192,224,256,288,320,352,384,416,448,480},{8,40,72,1..., dimensions={0} | all-to-all | bytes 786432 | tf_op jit(solution)/shard_map/all_to_all | solution.py:289
  97.2 0.7 shard_map.88
  (39 shorter events, 0.6 us)
Async XLA Ops:
  0.6 0.8 copy-start.4
  2.5 3.1 %collective-permute-start = (bf16[2,2,24,256]{3,2,0,1:T(8,128)(2,1)S(1)}, bf16[2,2,24,256]{3,2,0,1:T(8,128)(2,1)S(1)}, u32[]{:S(2)}, u32[]{:S(2)}) collective-permute-start(bf16[2,2,24,256]{3,2,0,1:T(8,128)(2,1)S(1)} %get-tuple-element.28), channel_id=1, source_target_pairs={{0,1},{1,0},{2,3},{3,2},{4,5},{5,4},{6,7},{7,6},{8,9},{9,8},{10,11... | collective-permute-start | bytes 147464 | tf_op jit(solution)/shard_map/ppermute | solution.py:263
  5.7 9.9 %collective-permute-start.1 = (bf16[2,2,24,256]{3,2,1,0:T(8,128)(2,1)S(1)}, bf16[2,2,24,256]{3,2,1,0:T(8,128)(2,1)S(1)}, u32[]{:S(2)}, u32[]{:S(2)}) collective-permute-start(bf16[2,2,24,256]{3,2,1,0:T(8,128)(2,1)S(1)} %get-tuple-element.26), channel_id=1, source_target_pairs={{0,2},{1,7},{2,0},{3,5},{4,6},{5,3},{6,4},{7,1},{8,10},{9,15},{10,... | collective-permute-start | bytes 147464 | tf_op jit(solution)/shard_map/ppermute | solution.py:263
  15.6 9.1 %copy-start = (s32[192]{0:T(256)S(1)}, s32[192]{0:T(256)}, u32[]{:S(2)}) copy-start(s32[192]{0:T(256)} %docs_ref.3) | copy-start | bytes 2308
  15.6 11.2 %collective-permute-start.2 = (bf16[2,2,24,256]{3,2,1,0:T(8,128)(2,1)S(1)}, bf16[2,2,24,256]{3,2,1,0:T(8,128)(2,1)S(1)}, u32[]{:S(2)}, u32[]{:S(2)}) collective-permute-start(bf16[2,2,24,256]{3,2,1,0:T(8,128)(2,1)S(1)} %get-tuple-element.24), channel_id=1, source_target_pairs={{0,6},{1,3},{2,4},{3,1},{4,2},{5,7},{6,0},{7,5},{8,14},{9,11},{10,... | collective-permute-start | bytes 147464 | tf_op jit(solution)/shard_map/ppermute | solution.py:263
  27.0 8.4 %collective-permute-start.3 = (bf16[200,256]{1,0:T(8,128)(2,1)S(1)}, bf16[200,256]{1,0:T(8,128)(2,1)S(1)}, u32[]{:S(2)}, u32[]{:S(2)}) collective-permute-start(bf16[200,256]{1,0:T(8,128)(2,1)S(1)} %get-tuple-element.20), channel_id=1, source_target_pairs={{0,32},{8,40},{16,48},{24,56},{32,64},{40,72},{48,80},{56,88},{64,... | collective-permute-start | bytes 307208 | tf_op jit(solution)/shard_map/ppermute | solution.py:277
  30.0 7.7 %collective-permute-start.4 = (bf16[200,256]{1,0:T(8,128)(2,1)S(1)}, bf16[200,256]{1,0:T(8,128)(2,1)S(1)}, u32[]{:S(2)}, u32[]{:S(2)}) collective-permute-start(bf16[200,256]{1,0:T(8,128)(2,1)S(1)} %get-tuple-element.20), channel_id=1, source_target_pairs={{0,64},{8,72},{16,80},{24,88},{32,96},{40,104},{48,112},{56,120},{... | collective-permute-start | bytes 307208 | tf_op jit(solution)/shard_map/ppermute | solution.py:277
  38.8 14.4 %copy-start.3 = (bf16[1,192,8,128]{3,2,1,0:T(8,128)(2,1)S(1)}, bf16[1,192,8,128]{3,2,1,0:T(8,128)(2,1)}, u32[]{:S(2)}) copy-start(bf16[1,192,8,128]{3,2,1,0:T(8,128)(2,1)} %param.10) | copy-start | bytes 1179652
  38.8 14.4 %all-to-all-start = ((bf16[4,2,200,256]{3,2,1,0:T(8,128)(2,1)}), bf16[4,2,200,256]{3,2,1,0:T(8,128)(2,1)S(1)}, u32[]{:S(2)}, u32[]{:S(2)}) async-start(bf16[4,2,200,256]{3,2,1,0:T(8,128)(2,1)} %pad_maximum_fusion), calls=%async_computation | async-start | bytes 1638400 | tf_op jit(solution)/shard_map/all_to_all | solution.py:280
  43.2 10.0 %copy-start.1 = (bf16[1,192,8,128]{3,2,1,0:T(8,128)(2,1)S(1)}, bf16[1,192,8,128]{3,2,1,0:T(8,128)(2,1)}, u32[]{:S(2)}) copy-start(bf16[1,192,8,128]{3,2,1,0:T(8,128)(2,1)} %param.11) | copy-start | bytes 1179652
  43.2 10.0 %copy-start.2 = (bf16[1,192,8,128]{3,2,1,0:T(8,128)(2,1)S(1)}, bf16[1,192,8,128]{3,2,1,0:T(8,128)(2,1)}, u32[]{:S(2)}) copy-start(bf16[1,192,8,128]{3,2,1,0:T(8,128)(2,1)} %param.6) | copy-start | bytes 1179652
  58.0 13.5 %all-to-all-start.1 = ((bf16[4,9,48,256]{3,2,1,0:T(8,128)(2,1)}), bf16[4,9,48,256]{3,2,1,0:T(8,128)(2,1)S(1)}, u32[]{:S(2)}, u32[]{:S(2)}) async-start(bf16[4,9,48,256]{3,2,1,0:T(8,128)(2,1)} %get-tuple-element.9), calls=%async_computation.1 | async-start | bytes 1769472 | tf_op jit(solution)/shard_map/all_to_all | solution.py:287

commit v4 on v3

v4 whole, which is shorter than its diff:
```python
import functools
import jax
import jax.numpy as jnp
from jax import lax
from jax.experimental import pallas as pl
from jax.experimental.pallas import tpu as pltpu
from jax.sharding import PartitionSpec as P

F32, BF16 = jnp.float32, jnp.bfloat16
TOK = 192
BACK = 9
KB = 576
ROWS = 1536
HEADS = 8
LOG2E = 1.4426950408889634
NEG = -1e30
SCALE2 = (128.0 ** -0.5) * LOG2E
PAY = 200
NT = (((1,), (1,)), ((), ()))
TN = (((0,), (0,)), ((), ()))


ORDER = ((8, 4, 0), (3, 2, 1), (7, 6, 5))


def keys_of(g):
    return pl.ds(pl.multiple_of(g * KB, KB), KB)


def load_window(where_ref, qdoc_ref, own_ref, recv_ref, kwin, vwin, ids_scr, start_scr, groups):
    block = where_ref[0]
    x = lax.rem(block, 4)
    ids_scr[...] = jnp.full_like(ids_scr, 100.0)
    lane = lax.broadcasted_iota(jnp.int32, (1, 256), 1)
    back = lax.broadcasted_iota(jnp.int32, (16, 1), 0)
    exists = jnp.zeros((16, 1), jnp.bool_)
    for g in groups:
        for b, k in enumerate(ORDER[g]):
            if k % 4 == 0:
                src = own_ref.at[k // 4]
            else:
                src = recv_ref.at[lax.rem(x - k + 8, 4), k // 4]
            row = g * 3 + b
            kwin[row * TOK:(row + 1) * TOK, :] = src[0:TOK, 0:128]
            if vwin is not None:
                vwin[row * TOK:(row + 1) * TOK, :] = src[0:TOK, 128:256]
            ids = src[TOK:TOK + 8, :].astype(F32)[0:1]
            ids_scr[row:row + 1, :] = jnp.where(lane < TOK, ids, 100.0)
            exists = exists | ((back == row) & (block >= k))
    ids = ids_scr[...]
    doc = qdoc_ref[...]
    start = jnp.zeros((16, ROWS), F32)
    for d in range(1, 4):
        count = jnp.sum(jnp.where(ids < d - 0.5, 1.0, 0.0), axis=1, keepdims=True)
        start = jnp.where(doc == d, count, start)
    start_scr[...] = jnp.where(exists, start, float(TOK)).astype(jnp.int32)


def masked_scores(key, q, start_scr, g, own):
    s = lax.dot_general(key, q, NT, preferred_element_type=F32) * SCALE2
    kp = lax.broadcasted_iota(jnp.int32, (TOK, ROWS), 0)
    parts = []
    for b in range(3):
        allowed = kp >= start_scr[pl.ds(g * 3 + b, 1), :]
        if own and b == 2:
            allowed = allowed & (kp <= lax.broadcasted_iota(jnp.int32, (1, ROWS), 1) // HEADS)
        parts.append(jnp.where(allowed, s[b * TOK:(b + 1) * TOK], NEG))
    return jnp.concatenate(parts)


def groups_used(start_scr):
    near = jnp.min(start_scr[5:6, :].astype(F32)) < TOK - 0.5
    far = jnp.min(start_scr[8:9, :].astype(F32)) < TOK - 0.5
    return 1 + near.astype(jnp.int32) + far.astype(jnp.int32)


def local_kernel(
    where_ref, qdoc_ref, q_ref, do_ref, o_ref, own_ref, t_ref, m_ref, l_ref, delta_ref, kwin, ids_scr, start_scr
):
    load_window(where_ref, qdoc_ref, own_ref, None, kwin, None, ids_scr, start_scr, (0,))
    t = masked_scores(kwin[...], q_ref[...], start_scr, 0, True)
    t_ref[...] = t
    t = t.reshape(KB // 8, 8, ROWS)
    top = jnp.max(t, axis=0)
    m_ref[...] = top
    l_ref[...] = jnp.sum(jnp.exp2(t - top), axis=0)
    delta_ref[...] = jnp.sum((do_ref[...].astype(F32) * o_ref[...].astype(F32)).T, axis=0, keepdims=True)


def key_value_kernel(
    where_ref, qdoc_ref, q_ref, do_ref, t_ref, m_ref, l_ref, delta_ref, own_ref, recv_ref,
    dkv_ref, stat_ref, kwin, vwin, t_scr, m_scr, l_scr, ids_scr, start_scr,
):
    load_window(where_ref, qdoc_ref, own_ref, recv_ref, kwin, vwin, ids_scr, start_scr, (0, 1, 2))
    used = groups_used(start_scr)
    m_scr[...] = m_ref[...]
    l_scr[...] = l_ref[...]

    def score_step(g, unused):
        t = masked_scores(kwin[keys_of(g), :], q_ref[...], start_scr, g, False)
        t_scr[keys_of(g - 1), :] = t
        t = t.reshape(KB // 8, 8, ROWS)
        old = m_scr[...]
        top = jnp.maximum(old, jnp.max(t, axis=0))
        m_scr[...] = top
        l_scr[...] = l_scr[...] * jnp.exp2(old - top) + jnp.sum(jnp.exp2(t - top), axis=0)
        return unused

    lax.fori_loop(1, used, score_step, 0)
    top = jnp.max(m_scr[...], axis=0, keepdims=True)
    total = jnp.sum(l_scr[...] * jnp.exp2(m_scr[...] - top), axis=0, keepdims=True)
    stat_ref[...] = top + jnp.log(total) * LOG2E

    def grad_step(g, t, blocks):
        q, do = q_ref[...], do_ref[...]
        prob = jnp.exp2(t - stat_ref[...])
        dp = lax.dot_general(vwin[keys_of(g), :], do, NT, preferred_element_type=F32)
        ds = (prob * (dp - delta_ref[...])).astype(BF16)
        dv = jnp.dot(prob.astype(BF16), do, preferred_element_type=F32)
        dk = jnp.dot(ds, q, preferred_element_type=F32)
        for b, back in enumerate(blocks):
            for r in range(4):
                part = slice(b * TOK + r * 48, b * TOK + r * 48 + 48)
                dkv_ref[r, back, :, 0:128] = dk[part].astype(BF16)
                dkv_ref[r, back, :, 128:256] = dv[part].astype(BF16)

    grad_step(0, t_ref[...], ORDER[0])

    def later_step(g, unused):
        grad_step(g, t_scr[keys_of(g - 1), :], [4 * g - 1 - b for b in range(3)])
        return unused

    lax.fori_loop(1, used, later_step, 0)

    def clear_step(g, unused):
        for b in range(3):
            for r in range(4):
                dkv_ref[r, 4 * g - 1 - b] = jnp.zeros((48, 256), BF16)
        return unused

    lax.fori_loop(used, 3, clear_step, 0)


def query_kernel(
    where_ref, qdoc_ref, q_ref, do_ref, stat_ref, delta_ref, own_ref, recv_ref,
    dq_ref, kwin, vwin, dq_acc, ids_scr, start_scr,
):
    load_window(where_ref, qdoc_ref, own_ref, recv_ref, kwin, vwin, ids_scr, start_scr, (0, 1, 2))

    def query_step(g, own):
        key = kwin[keys_of(g), :]
        prob = jnp.exp2(masked_scores(key, q_ref[...], start_scr, g, own) - stat_ref[...])
        dp = lax.dot_general(vwin[keys_of(g), :], do_ref[...], NT, preferred_element_type=F32)
        ds = (prob * (dp - delta_ref[...])).astype(BF16)
        return lax.dot_general(key, ds, TN, preferred_element_type=F32)

    dq_acc[...] = query_step(0, True)

    def later_step(g, unused):
        dq_acc[...] += query_step(g, False)
        return unused

    lax.fori_loop(1, groups_used(start_scr), later_step, 0)
    dq_ref[...] = (dq_acc[...].T * (128.0 ** -0.5)).astype(BF16)


VMEM_SPEC = pl.BlockSpec(memory_space=pltpu.VMEM)
SMEM_SPEC = pl.BlockSpec(memory_space=pltpu.SMEM)


def window_scratch():
    return [pltpu.VMEM((16, 256), F32), pltpu.VMEM((16, ROWS), jnp.int32)]


def local_scores(where, qdoc, q, do, o, own):
    return pl.pallas_call(
        local_kernel,
        out_shape=(
            jax.ShapeDtypeStruct((KB, ROWS), F32),
            jax.ShapeDtypeStruct((8, ROWS), F32),
            jax.ShapeDtypeStruct((8, ROWS), F32),
            jax.ShapeDtypeStruct((1, ROWS), F32),
        ),
        in_specs=[SMEM_SPEC] + [VMEM_SPEC] * 5,
        out_specs=(VMEM_SPEC,) * 4,
        scratch_shapes=[pltpu.VMEM((KB, 128), BF16)] + window_scratch(),
        compiler_params=pltpu.CompilerParams(vmem_limit_bytes=24 << 20),
        cost_estimate=pl.CostEstimate(flops=1 << 29, bytes_accessed=5 << 20, transcendentals=1 << 20),
    )(where, qdoc, q, do, o, own)


def key_value_grads(where, qdoc, q, do, local, own, recv):
    return pl.pallas_call(
        key_value_kernel,
        out_shape=(
            jax.ShapeDtypeStruct((4, BACK, 48, 256), BF16),
            jax.ShapeDtypeStruct((1, ROWS), F32),
        ),
        in_specs=[SMEM_SPEC] + [VMEM_SPEC] * 9,
        out_specs=(VMEM_SPEC, VMEM_SPEC),
        scratch_shapes=[
            pltpu.VMEM((BACK * TOK, 128), BF16),
            pltpu.VMEM((BACK * TOK, 128), BF16),
            pltpu.VMEM((2 * KB, ROWS), F32),
            pltpu.VMEM((8, ROWS), F32),
            pltpu.VMEM((8, ROWS), F32),
        ] + window_scratch(),
        compiler_params=pltpu.CompilerParams(vmem_limit_bytes=32 << 20),
        cost_estimate=pl.CostEstimate(flops=4 << 30, bytes_accessed=3 << 20, transcendentals=2 << 20),
    )(where, qdoc, q, do, *local, own, recv)


def query_grads(where, qdoc, q, do, stat, delta, own, recv):
    return pl.pallas_call(
        query_kernel,
        out_shape=jax.ShapeDtypeStruct((ROWS, 128), BF16),
        in_specs=[SMEM_SPEC] + [VMEM_SPEC] * 7,
        out_specs=VMEM_SPEC,
        scratch_shapes=[
            pltpu.VMEM((BACK * TOK, 128), BF16),
            pltpu.VMEM((BACK * TOK, 128), BF16),
            pltpu.VMEM((128, ROWS), F32),
        ] + window_scratch(),
        compiler_params=pltpu.CompilerParams(vmem_limit_bytes=32 << 20),
        cost_estimate=pl.CostEstimate(flops=3 << 30, bytes_accessed=3 << 20, transcendentals=2 << 20),
    )(where, qdoc, q, do, stat, delta, own, recv)


def attention_grads(where, qdoc, q, do, o, own, recv):
    local = local_scores(where, qdoc, q, do, o, own)
    recv, local = lax.optimization_barrier((recv, local))
    dkv, stat = key_value_grads(where, qdoc, q, do, local, own, recv)
    return query_grads(where, qdoc, q, do, stat, local[3], own, recv), dkv


def sum_kernel(group_ref, part_ref, out_ref):
    first = 4 * group_ref[0] - 8
    out_ref[...] = jnp.zeros_like(out_ref)
    for j in range(12):

        @pl.when(first + j >= 0)
        def _():
            terms = [part_ref[xs, 8 + xs - j].astype(F32) for xs in range(4) if 0 <= 8 + xs - j < BACK]
            out_ref[jnp.maximum(first + j, 0)] = sum(terms[1:], terms[0]).astype(BF16)


def sum_terms(group, part):
    return pl.pallas_call(
        sum_kernel,
        out_shape=jax.ShapeDtypeStruct((16, 48, 256), BF16),
        in_specs=[SMEM_SPEC, VMEM_SPEC],
        out_specs=VMEM_SPEC,
        compiler_params=pltpu.CompilerParams(vmem_limit_bytes=8 << 20),
        cost_estimate=pl.CostEstimate(flops=1 << 20, bytes_accessed=1 << 20, transcendentals=0),
    )(group, part)


def finish_kernel(last_ref, dk_ref, dv_ref):
    total = jnp.sum(last_ref[...].astype(F32), axis=0)
    dk_ref[...] = (total[:, 0:128] * (128.0 ** -0.5)).astype(BF16)
    dv_ref[...] = total[:, 128:256].astype(BF16)


def finish(last):
    return pl.pallas_call(
        finish_kernel,
        out_shape=(jax.ShapeDtypeStruct((48, 128), BF16),) * 2,
        in_specs=[VMEM_SPEC],
        out_specs=(VMEM_SPEC, VMEM_SPEC),
        compiler_params=pltpu.CompilerParams(vmem_limit_bytes=8 << 20),
        cost_estimate=pl.CostEstimate(flops=1 << 18, bytes_accessed=1 << 19, transcendentals=0),
    )(last)


X_GROUPS = [[4 * a + x for x in range(4)] for a in range(4)]


def on_device(queries, keys, values, doc_ids, output_gradient, attention_output):
    block = lax.axis_index("seq")
    a, x = block // 4, lax.rem(block, 4)
    tp = lax.axis_index("tp")
    core, half = tp % 2 == 1, tp >= 4
    near = ((tp // 2) % 2 == 1) != half
    bits = (half, near, core)

    def by_label(array):
        for axis, bit in enumerate(bits):
            array = jnp.where(bit, jnp.flip(array, axis), array)
        return array

    def relabel(array):
        return jnp.stack([array[0:2], jnp.flip(array[2:4], 0)])

    def by_core(array):
        return jnp.where(core, jnp.swapaxes(array, 0, 1), array)

    def swap(array, flip0, flip1):
        return lax.ppermute(array, "tp", [(i, i ^ (flip1 if i % 2 else flip0)) for i in range(8)])

    kv = jnp.concatenate([keys, values], axis=2).transpose(1, 0, 2).reshape(4, 2, 24, 256)
    part = by_label(relabel(kv))
    got = swap(part[:, :, 1], 1, 1)
    part = by_core(jnp.stack([part[:, :, 0], got], axis=2))
    got = swap(part[:, 1], 2, 6)
    part = jnp.stack([part[:, 0], got], axis=1)
    got = swap(part[1], 6, 2)
    part = by_label(by_core(jnp.stack([part[0], got])))
    kv = jnp.concatenate([part[0], jnp.flip(part[1], 0)]).reshape(TOK, 256)
    ids = jnp.pad(doc_ids.astype(BF16), (0, 64))
    tail = jnp.concatenate([ids[None], jnp.zeros((PAY - TOK - 1, 256), BF16)], axis=0)
    pay = jnp.concatenate([kv, tail], axis=0)
    back = [lax.ppermute(pay, "seq", [(i, i + k) for i in range(16 - k)]) for k in (4, 8)]
    own = jnp.stack([pay] + back)
    send = jnp.stack([jnp.where(x < dest, own[0:2], own[1:3]) for dest in range(4)])
    recv = lax.all_to_all(send, "seq", split_axis=0, concat_axis=0, tiled=True, axis_index_groups=X_GROUPS)
    qdoc = jnp.repeat(doc_ids, HEADS)[None]
    dq, dkv = attention_grads(
        block.reshape(1), qdoc,
        queries.reshape(ROWS, 128), output_gradient.reshape(ROWS, 128), attention_output.reshape(ROWS, 128),
        own, recv,
    )
    part = lax.all_to_all(dkv, "seq", split_axis=0, concat_axis=0, tiled=True, axis_index_groups=X_GROUPS)
    part, dq = lax.optimization_barrier((part, dq))
    last = lax.all_to_all(
        sum_terms(a.reshape(1), part), ("head", "seq"), split_axis=0, concat_axis=0, tiled=True,
        axis_index_groups=[[16 * h + 4 * z + xs for h in range(4) for z in range(4)] for xs in range(4)],
    )
    grad_keys, grad_values = finish(last)
    grad_keys, grad_values = grad_keys[:, None], grad_values[:, None]
    return dq.reshape(1, TOK, HEADS, 128), grad_keys, grad_values


def solution(mesh):
    placed = (
        P("head", "seq", "tp", None),
        P(("seq", "tp"), None, None),
        P(("seq", "tp"), None, None),
        P("seq"),
        P("head", "seq", "tp", None),
        P("head", "seq", "tp", None),
    )
    return jax.shard_map(
        on_device,
        mesh=mesh,
        in_specs=placed,
        out_specs=(
            P("head", "seq", "tp", None),
            P(("head", "seq"), "tp", None),
            P(("head", "seq"), "tp", None),
        ),
        check_vma=False,
    )
```

time: 98.5 us -> 96.6 us (0.981)
  waiting for transfers between devices: 25.5 us -> 22.3 us
  blocking collectives: 25.7 us -> 22.6 us
  local copies, waits for them, and re-layouts: 1.22 us -> 4.23 us
  starting transfers between devices: 33.4 us -> 35.2 us
  Pallas kernels: 8.89 us -> 7.85 us
    all_to_all x1, waiting for transfers between devices: 9.71 us -> 6.59 us  [on_device(): lax.all_to_all(send, 'seq', split_axis=0, concat_axis=0, tiled=True, axis...]
    all_to_all x1, blocking collectives: 25.7 us -> 22.6 us  [on_device(): lax.all_to_all(sum_terms(a.reshape(1), part), ('head', 'seq'), split_axis...]
    unnamed x10 -> x12, local copies, waits for them, and re-layouts: 0.77 us -> 3.78 us
    pallas_call x1, Pallas kernels: 4.8 us -> 2.9 us  [key_value_grads(): pl.pallas_call(key_value_kernel, out_shape=(jax.ShapeDtypeStruct((4, BACK...]
    all_to_all x1, starting transfers between devices: 3.5 us -> 5.34 us  [on_device(): lax.all_to_all(dkv, 'seq', split_axis=0, concat_axis=0, tiled=True, axis_...]
    pallas_call x0 -> x1, Pallas kernels: none -> 1.34 us  [local_scores(): pl.pallas_call(local_kernel, out_shape=(jax.ShapeDtypeStruct((KB, ROWS),...]
  transfers between devices with their start and end apart: 7 -> 7, of which waited for: 6 -> 6; matrix products, arithmetic and copies ran while one was open for 0% -> 1% of each run, Pallas kernels for 3% -> 4%
where the time goes in v4:
time: 96.6 us; the launch traced here: 96.1 us
  starting transfers between devices  35.2 us (36%)
  blocking collectives  22.6 us (23%)
  waiting for transfers between devices  22.3 us (23%)
  Pallas kernels  7.85 us (8%)
  local copies, waits for them, and re-layouts  4.23 us (4%)
  other arithmetic  2.92 us (3%)
  between operations  0.99 us (1%)
    all_to_all x1, blocking collectives, on_device(): lax.all_to_all(sum_terms(a.reshape(1), part), ('head', 'seq'), split_axis...  22.6 us
    ppermute x3, starting transfers between devices, swap(): lax.ppermute(array, 'tp', [(i, i ^ (flip1 if i % 2 else flip0)) for i in...  17 us
    ppermute x2, starting transfers between devices, on_device(): lax.ppermute(pay, 'seq', [(i, i + k) for i in range(16 - k)])  8.55 us
    all_to_all x1, waiting for transfers between devices, on_device(): lax.all_to_all(dkv, 'seq', split_axis=0, concat_axis=0, tiled=True, axis_...  7.17 us
    all_to_all x1, waiting for transfers between devices, on_device(): lax.all_to_all(send, 'seq', split_axis=0, concat_axis=0, tiled=True, axis...  6.59 us
    ppermute x3, waiting for transfers between devices, swap(): lax.ppermute(array, 'tp', [(i, i ^ (flip1 if i % 2 else flip0)) for i in...  6.33 us
    all_to_all x1, starting transfers between devices, on_device(): lax.all_to_all(dkv, 'seq', split_axis=0, concat_axis=0, tiled=True, axis_...  5.34 us
    all_to_all x1, starting transfers between devices, on_device(): lax.all_to_all(send, 'seq', split_axis=0, concat_axis=0, tiled=True, axis...  4.29 us
  transfers between devices with their start and end apart: 7, of which 6 were waited for; matrix products, arithmetic and copies ran while one was open for 1% of the time, Pallas kernels for 4%

profile of v4, /device:TPU:128, one launch (start us, length us, event | category | flops | bytes accessed | tf_op | source)
XLA Modules:
  0.0 96.1 jit_solution(4836985144421866955)
XLA Ops:
  0.7 0.8 maximum_bitcast_fusion
  1.8 1.9 %collective-permute-start = (bf16[2,2,24,256]{3,2,0,1:T(8,128)(2,1)S(1)}, bf16[2,2,24,256]{3,2,0,1:T(8,128)(2,1)S(1)}, u32[]{:S(2)}, u32[]{:S(2)}) collective-permute-start(bf16[2,2,24,256]{3,2,0,1:T(8,128)(2,1)S(1)} %get-tuple-element.46), channel_id=1, source_target_pairs={{0,1},{1,0},{2,3},{3,2},{4,5},{5,4},{6,7},{7,6},{8,9},{9,8},{10,11... | collective-permute-start | bytes 147464 | tf_op jit(solution)/shard_map/ppermute | solution.py:298
  3.7 1.2 %collective-permute-done = bf16[2,2,24,256]{3,2,0,1:T(8,128)(2,1)S(1)} collective-permute-done((bf16[2,2,24,256]{3,2,0,1:T(8,128)(2,1)S(1)}, bf16[2,2,24,256]{3,2,0,1:T(8,128)(2,1)S(1)}, u32[]{:S(2)}, u32[]{:S(2)}) %collective-permute-start) | collective-permute-done | bytes 49184 | tf_op jit(solution)/shard_map/ppermute | solution.py:298
  5.0 6.0 %collective-permute-start.1 = (bf16[2,2,24,256]{3,2,1,0:T(8,128)(2,1)S(1)}, bf16[2,2,24,256]{3,2,1,0:T(8,128)(2,1)S(1)}, u32[]{:S(2)}, u32[]{:S(2)}) collective-permute-start(bf16[2,2,24,256]{3,2,1,0:T(8,128)(2,1)S(1)} %get-tuple-element.44), channel_id=1, source_target_pairs={{0,2},{1,7},{2,0},{3,5},{4,6},{5,3},{6,4},{7,1},{8,10},{9,15},{10,... | collective-permute-start | bytes 147464 | tf_op jit(solution)/shard_map/ppermute | solution.py:298
  11.0 3.9 %collective-permute-done.1 = bf16[2,2,24,256]{3,2,1,0:T(8,128)(2,1)S(1)} collective-permute-done((bf16[2,2,24,256]{3,2,1,0:T(8,128)(2,1)S(1)}, bf16[2,2,24,256]{3,2,1,0:T(8,128)(2,1)S(1)}, u32[]{:S(2)}, u32[]{:S(2)}) %collective-permute-start.1) | collective-permute-done | bytes 49184 | tf_op jit(solution)/shard_map/ppermute | solution.py:298
  14.9 9.1 %collective-permute-start.2 = (bf16[2,2,24,256]{3,2,1,0:T(8,128)(2,1)S(1)}, bf16[2,2,24,256]{3,2,1,0:T(8,128)(2,1)S(1)}, u32[]{:S(2)}, u32[]{:S(2)}) collective-permute-start(bf16[2,2,24,256]{3,2,1,0:T(8,128)(2,1)S(1)} %get-tuple-element.42), channel_id=1, source_target_pairs={{0,6},{1,3},{2,4},{3,1},{4,2},{5,7},{6,0},{7,5},{8,14},{9,11},{10,... | collective-permute-start | bytes 147464 | tf_op jit(solution)/shard_map/ppermute | solution.py:298
  24.0 0.7 convert_element_type.5
  24.8 1.3 %collective-permute-done.2 = bf16[2,2,24,256]{3,2,1,0:T(8,128)(2,1)S(1)} collective-permute-done((bf16[2,2,24,256]{3,2,1,0:T(8,128)(2,1)S(1)}, bf16[2,2,24,256]{3,2,1,0:T(8,128)(2,1)S(1)}, u32[]{:S(2)}, u32[]{:S(2)}) %collective-permute-start.2) | collective-permute-done | bytes 49184 | tf_op jit(solution)/shard_map/ppermute | solution.py:298
  26.3 3.1 %collective-permute-start.3 = (bf16[200,256]{1,0:T(8,128)(2,1)S(1)}, bf16[200,256]{1,0:T(8,128)(2,1)S(1)}, u32[]{:S(2)}, u32[]{:S(2)}) collective-permute-start(bf16[200,256]{1,0:T(8,128)(2,1)S(1)} %get-tuple-element.38), channel_id=1, source_target_pairs={{0,32},{8,40},{16,48},{24,56},{32,64},{40,72},{48,80},{56,88},{64,... | collective-permute-start | bytes 307208 | tf_op jit(solution)/shard_map/ppermute | solution.py:312
  29.5 5.4 %collective-permute-start.4 = (bf16[200,256]{1,0:T(8,128)(2,1)S(1)}, bf16[200,256]{1,0:T(8,128)(2,1)S(1)}, u32[]{:S(2)}, u32[]{:S(2)}) collective-permute-start(bf16[200,256]{1,0:T(8,128)(2,1)S(1)} %get-tuple-element.38), channel_id=1, source_target_pairs={{0,64},{8,72},{16,80},{24,88},{32,96},{40,104},{48,112},{56,120},{... | collective-permute-start | bytes 307208 | tf_op jit(solution)/shard_map/ppermute | solution.py:312
  34.9 2.2 %collective-permute-done.4 = bf16[200,256]{1,0:T(8,128)(2,1)S(1)} collective-permute-done((bf16[200,256]{1,0:T(8,128)(2,1)S(1)}, bf16[200,256]{1,0:T(8,128)(2,1)S(1)}, u32[]{:S(2)}, u32[]{:S(2)}) %collective-permute-start.4) | collective-permute-done | bytes 102432 | tf_op jit(solution)/shard_map/ppermute | solution.py:312
  37.2 1.0 %pad_maximum_fusion = bf16[4,2,200,256]{3,2,1,0:T(8,128)(2,1)} fusion(bf16[1,2,200,256]{3,2,1,0:T(8,128)(2,1)S(1)} %broadcast_select_fusion, bf16[1,2,200,256]{3,2,1,0:T(8,128)(2,1)S(1)} %get-tuple-element.35, bf16[1,2,200,256]{3,2,1,0:T(8,128)(2,1)S(1)} %get-tuple-element.34, bf16[1,2,200,256]{3,2,1,0:T(8,128)(2,1)S(1)} %get-tuple-element.33), kind=kLoop, calls=%fused_computation | loop fusion | flops 1228800 | bytes 1638400 | tf_op jit(solution)/shard_map/stack | solution.py:314
  38.2 4.3 %all-to-all-start = ((bf16[4,2,200,256]{3,2,1,0:T(8,128)(2,1)}), bf16[4,2,200,256]{3,2,1,0:T(8,128)(2,1)S(1)}, u32[]{:S(2)}, u32[]{:S(2)}) async-start(bf16[4,2,200,256]{3,2,1,0:T(8,128)(2,1)} %pad_maximum_fusion), calls=%async_computation | async-start | bytes 1638400 | tf_op jit(solution)/shard_map/all_to_all | solution.py:315
  42.6 0.1 broadcast_in_dim_reshape.3.qdoc_ref
  42.8 1.3 %shard_map.85 = (f32[576,1536]{1,0:T(8,128)S(1)}, f32[8,1536]{1,0:T(8,128)S(1)}, f32[8,1536]{1,0:T(8,128)S(1)}, f32[1,1536]{1,0:T(1,128)S(1)}) custom-call(s32[1]{0:T(128)} %bitcast.where_ref, s32[1,1536]{1,0:T(1,128)S(1)} %broadcast_in_dim_reshape.3.qdoc_ref, bf16[1536,128]{1,0:T(8,128)(2,1)S(1)} %bitcast.49, bf16[1536,128]{1,0:T(8,128)(2,1)S(1)} %bitcast.52, ...), custom_call_target="tpu_custom_call" | custom-call | flops 536870912 | bytes 5242880 | tf_op jit(solution)/shard_map/pallas_call | solution.py:176
  44.1 1.8 %copy-done.3 = f32[576,1536]{1,0:T(8,128)} copy-done((f32[576,1536]{1,0:T(8,128)}, f32[576,1536]{1,0:T(8,128)S(1)}, u32[]{:S(2)}) %copy-start.3) | copy-done | bytes 3538968
  45.9 6.6 %all-to-all-done.recv_ref = bf16[4,2,200,256]{3,2,1,0:T(8,128)(2,1)S(1)} async-done(((bf16[4,2,200,256]{3,2,1,0:T(8,128)(2,1)}), bf16[4,2,200,256]{3,2,1,0:T(8,128)(2,1)S(1)}, u32[]{:S(2)}, u32[]{:S(2)}) %all-to-all-start) | async-done | bytes 819232 | tf_op jit(solution)/shard_map/all_to_all | solution.py:315
  52.5 2.0 %copy-done.4 = f32[576,1536]{1,0:T(8,128)S(1)} copy-done((f32[576,1536]{1,0:T(8,128)S(1)}, f32[576,1536]{1,0:T(8,128)}, u32[]{:S(2)}) %copy-start.4) | copy-done | bytes 3538968
  54.5 2.9 %shard_map.86 = (bf16[4,9,48,256]{3,2,1,0:T(8,128)(2,1)}, f32[1,1536]{1,0:T(1,128)S(1)}) custom-call(s32[1]{0:T(128)} %bitcast.where_ref, s32[1,1536]{1,0:T(1,128)S(1)} %broadcast_in_dim_reshape.3.qdoc_ref, bf16[1536,128]{1,0:T(8,128)(2,1)S(1)} %bitcast.50, bf16[1536,128]{1,0:T(8,128)(2,1)S(1)} %bitcast.53, f32[576,1536]{1,0:T(8,128)S(1)} %copy-done.4, ...), custom_call_target="tpu_custom_call" | custom-call | flops 4294967296 | bytes 3145728 | tf_op jit(solution)/shard_map/pallas_call | solution.py:193
  57.4 5.3 %all-to-all-start.1 = ((bf16[4,9,48,256]{3,2,1,0:T(8,128)(2,1)}), bf16[4,9,48,256]{3,2,1,0:T(8,128)(2,1)S(1)}, u32[]{:S(2)}, u32[]{:S(2)}) async-start(bf16[4,9,48,256]{3,2,1,0:T(8,128)(2,1)} %get-tuple-element.27), calls=%async_computation.1 | async-start | bytes 1769472 | tf_op jit(solution)/shard_map/all_to_all | solution.py:322
  62.7 2.8 %shard_map.87 = bf16[1536,128]{1,0:T(8,128)(2,1)} custom-call(s32[1]{0:T(128)} %bitcast.where_ref, s32[1,1536]{1,0:T(1,128)S(1)} %broadcast_in_dim_reshape.3.qdoc_ref, bf16[1536,128]{1,0:T(8,128)(2,1)S(1)} %bitcast.51, bf16[1536,128]{1,0:T(8,128)(2,1)S(1)} %bitcast.54, f32[1,1536]{1,0:T(1,128)S(1)} %get-tuple-element.28.stat_ref, ...), custom_call_target="tpu_custom_call" | custom-call | flops 3221225472 | bytes 3145728 | tf_op jit(solution)/shard_map/pallas_call | solution.py:214
  65.6 7.2 %all-to-all-done.1.part_ref = bf16[4,9,48,256]{3,2,1,0:T(8,128)(2,1)S(1)} async-done(((bf16[4,9,48,256]{3,2,1,0:T(8,128)(2,1)}), bf16[4,9,48,256]{3,2,1,0:T(8,128)(2,1)S(1)}, u32[]{:S(2)}, u32[]{:S(2)}) %all-to-all-start.1) | async-done | bytes 884768 | tf_op jit(solution)/shard_map/all_to_all | solution.py:322
  72.8 22.6 %all_to_all.15.last_ref = bf16[16,48,256]{2,1,0:T(8,128)(2,1)S(1)} all-to-all(bf16[16,48,256]{2,1,0:T(8,128)(2,1)S(1)} %shard_map.88), channel_id=1, replica_groups={{0,32,64,96,128,160,192,224,256,288,320,352,384,416,448,480},{8,40,72,1..., dimensions={0} | all-to-all | bytes 786432 | tf_op jit(solution)/shard_map/all_to_all | solution.py:324
  95.4 0.7 shard_map.89
  (42 shorter events, 0.9 us)
Async XLA Ops:
  1.8 3.1 %collective-permute-start = (bf16[2,2,24,256]{3,2,0,1:T(8,128)(2,1)S(1)}, bf16[2,2,24,256]{3,2,0,1:T(8,128)(2,1)S(1)}, u32[]{:S(2)}, u32[]{:S(2)}) collective-permute-start(bf16[2,2,24,256]{3,2,0,1:T(8,128)(2,1)S(1)} %get-tuple-element.46), channel_id=1, source_target_pairs={{0,1},{1,0},{2,3},{3,2},{4,5},{5,4},{6,7},{7,6},{8,9},{9,8},{10,11... | collective-permute-start | bytes 147464 | tf_op jit(solution)/shard_map/ppermute | solution.py:298
  4.9 37.6 %copy-start.5 = (s32[192]{0:T(256)S(1)}, s32[192]{0:T(256)}, u32[]{:S(2)}) copy-start(s32[192]{0:T(256)} %param.9) | copy-start | bytes 2308
  5.0 9.9 %collective-permute-start.1 = (bf16[2,2,24,256]{3,2,1,0:T(8,128)(2,1)S(1)}, bf16[2,2,24,256]{3,2,1,0:T(8,128)(2,1)S(1)}, u32[]{:S(2)}, u32[]{:S(2)}) collective-permute-start(bf16[2,2,24,256]{3,2,1,0:T(8,128)(2,1)S(1)} %get-tuple-element.44), channel_id=1, source_target_pairs={{0,2},{1,7},{2,0},{3,5},{4,6},{5,3},{6,4},{7,1},{8,10},{9,15},{10,... | collective-permute-start | bytes 147464 | tf_op jit(solution)/shard_map/ppermute | solution.py:298
  14.9 11.2 %collective-permute-start.2 = (bf16[2,2,24,256]{3,2,1,0:T(8,128)(2,1)S(1)}, bf16[2,2,24,256]{3,2,1,0:T(8,128)(2,1)S(1)}, u32[]{:S(2)}, u32[]{:S(2)}) collective-permute-start(bf16[2,2,24,256]{3,2,1,0:T(8,128)(2,1)S(1)} %get-tuple-element.42), channel_id=1, source_target_pairs={{0,6},{1,3},{2,4},{3,1},{4,2},{5,7},{6,0},{7,5},{8,14},{9,11},{10,... | collective-permute-start | bytes 147464 | tf_op jit(solution)/shard_map/ppermute | solution.py:298
  26.1 16.7 %copy-start = (bf16[1,192,8,128]{3,2,1,0:T(8,128)(2,1)S(1)}, bf16[1,192,8,128]{3,2,1,0:T(8,128)(2,1)}, u32[]{:S(2)}) copy-start(bf16[1,192,8,128]{3,2,1,0:T(8,128)(2,1)} %param.11) | copy-start | bytes 1179652
  26.1 16.7 %copy-start.1 = (bf16[1,192,8,128]{3,2,1,0:T(8,128)(2,1)S(1)}, bf16[1,192,8,128]{3,2,1,0:T(8,128)(2,1)}, u32[]{:S(2)}) copy-start(bf16[1,192,8,128]{3,2,1,0:T(8,128)(2,1)} %param.6) | copy-start | bytes 1179652
  26.1 16.7 %copy-start.2 = (bf16[1,192,8,128]{3,2,1,0:T(8,128)(2,1)S(1)}, bf16[1,192,8,128]{3,2,1,0:T(8,128)(2,1)}, u32[]{:S(2)}) copy-start(bf16[1,192,8,128]{3,2,1,0:T(8,128)(2,1)} %param.10) | copy-start | bytes 1179652
  26.3 8.6 %collective-permute-start.3 = (bf16[200,256]{1,0:T(8,128)(2,1)S(1)}, bf16[200,256]{1,0:T(8,128)(2,1)S(1)}, u32[]{:S(2)}, u32[]{:S(2)}) collective-permute-start(bf16[200,256]{1,0:T(8,128)(2,1)S(1)} %get-tuple-element.38), channel_id=1, source_target_pairs={{0,32},{8,40},{16,48},{24,56},{32,64},{40,72},{48,80},{56,88},{64,... | collective-permute-start | bytes 307208 | tf_op jit(solution)/shard_map/ppermute | solution.py:312
  29.5 7.7 %collective-permute-start.4 = (bf16[200,256]{1,0:T(8,128)(2,1)S(1)}, bf16[200,256]{1,0:T(8,128)(2,1)S(1)}, u32[]{:S(2)}, u32[]{:S(2)}) collective-permute-start(bf16[200,256]{1,0:T(8,128)(2,1)S(1)} %get-tuple-element.38), channel_id=1, source_target_pairs={{0,64},{8,72},{16,80},{24,88},{32,96},{40,104},{48,112},{56,120},{... | collective-permute-start | bytes 307208 | tf_op jit(solution)/shard_map/ppermute | solution.py:312
  38.2 14.3 %all-to-all-start = ((bf16[4,2,200,256]{3,2,1,0:T(8,128)(2,1)}), bf16[4,2,200,256]{3,2,1,0:T(8,128)(2,1)S(1)}, u32[]{:S(2)}, u32[]{:S(2)}) async-start(bf16[4,2,200,256]{3,2,1,0:T(8,128)(2,1)} %pad_maximum_fusion), calls=%async_computation | async-start | bytes 1638400 | tf_op jit(solution)/shard_map/all_to_all | solution.py:315
  44.1 1.8 %copy-start.3 = (f32[576,1536]{1,0:T(8,128)}, f32[576,1536]{1,0:T(8,128)S(1)}, u32[]{:S(2)}) copy-start(f32[576,1536]{1,0:T(8,128)S(1)} %get-tuple-element.22.t_ref) | copy-start | bytes 10616836
  52.5 2.0 %copy-start.4 = (f32[576,1536]{1,0:T(8,128)S(1)}, f32[576,1536]{1,0:T(8,128)}, u32[]{:S(2)}) copy-start(f32[576,1536]{1,0:T(8,128)} %copy-done.3) | copy-start | bytes 10616836
  57.4 15.4 %all-to-all-start.1 = ((bf16[4,9,48,256]{3,2,1,0:T(8,128)(2,1)}), bf16[4,9,48,256]{3,2,1,0:T(8,128)(2,1)S(1)}, u32[]{:S(2)}, u32[]{:S(2)}) async-start(bf16[4,9,48,256]{3,2,1,0:T(8,128)(2,1)} %get-tuple-element.27), calls=%async_computation.1 | async-start | bytes 1769472 | tf_op jit(solution)/shard_map/all_to_all | solution.py:322

commit v5 on v4

--- a/solution.py
+++ b/solution.py
@@ -75,11 +75,10 @@
 
 
 def local_kernel(
-    where_ref, qdoc_ref, q_ref, do_ref, o_ref, own_ref, t_ref, m_ref, l_ref, delta_ref, kwin, ids_scr, start_scr
+    where_ref, qdoc_ref, q_ref, do_ref, o_ref, own_ref, m_ref, l_ref, delta_ref, kwin, ids_scr, start_scr
 ):
     load_window(where_ref, qdoc_ref, own_ref, None, kwin, None, ids_scr, start_scr, (0,))
     t = masked_scores(kwin[...], q_ref[...], start_scr, 0, True)
-    t_ref[...] = t
     t = t.reshape(KB // 8, 8, ROWS)
     top = jnp.max(t, axis=0)
     m_ref[...] = top
@@ -88,7 +87,7 @@
 
 
 def key_value_kernel(
-    where_ref, qdoc_ref, q_ref, do_ref, t_ref, m_ref, l_ref, delta_ref, own_ref, recv_ref,
+    where_ref, qdoc_ref, q_ref, do_ref, m_ref, l_ref, delta_ref, own_ref, recv_ref,
     dkv_ref, stat_ref, kwin, vwin, t_scr, m_scr, l_scr, ids_scr, start_scr,
 ):
     load_window(where_ref, qdoc_ref, own_ref, recv_ref, kwin, vwin, ids_scr, start_scr, (0, 1, 2))
@@ -124,7 +123,7 @@
                 dkv_ref[r, back, :, 0:128] = dk[part].astype(BF16)
                 dkv_ref[r, back, :, 128:256] = dv[part].astype(BF16)
 
-    grad_step(0, t_ref[...], ORDER[0])
+    grad_step(0, masked_scores(kwin[keys_of(0), :], q_ref[...], start_scr, 0, True), ORDER[0])
 
     def later_step(g, unused):
         grad_step(g, t_scr[keys_of(g - 1), :], [4 * g - 1 - b for b in range(3)])
@@ -176,13 +175,12 @@
     return pl.pallas_call(
         local_kernel,
         out_shape=(
-            jax.ShapeDtypeStruct((KB, ROWS), F32),
             jax.ShapeDtypeStruct((8, ROWS), F32),
             jax.ShapeDtypeStruct((8, ROWS), F32),
             jax.ShapeDtypeStruct((1, ROWS), F32),
         ),
         in_specs=[SMEM_SPEC] + [VMEM_SPEC] * 5,
-        out_specs=(VMEM_SPEC,) * 4,
+        out_specs=(VMEM_SPEC,) * 3,
         scratch_shapes=[pltpu.VMEM((KB, 128), BF16)] + window_scratch(),
         compiler_params=pltpu.CompilerParams(vmem_limit_bytes=24 << 20),
         cost_estimate=pl.CostEstimate(flops=1 << 29, bytes_accessed=5 << 20, transcendentals=1 << 20),
@@ -196,7 +194,7 @@
             jax.ShapeDtypeStruct((4, BACK, 48, 256), BF16),
             jax.ShapeDtypeStruct((1, ROWS), F32),
         ),
-        in_specs=[SMEM_SPEC] + [VMEM_SPEC] * 9,
+        in_specs=[SMEM_SPEC] + [VMEM_SPEC] * 8,
         out_specs=(VMEM_SPEC, VMEM_SPEC),
         scratch_shapes=[
             pltpu.VMEM((BACK * TOK, 128), BF16),
@@ -230,7 +228,7 @@
     local = local_scores(where, qdoc, q, do, o, own)
     recv, local = lax.optimization_barrier((recv, local))
     dkv, stat = key_value_grads(where, qdoc, q, do, local, own, recv)
-    return query_grads(where, qdoc, q, do, stat, local[3], own, recv), dkv
+    return query_grads(where, qdoc, q, do, stat, local[2], own, recv), dkv
 
 
 def sum_kernel(group_ref, part_ref, out_ref):

time: 96.6 us -> 96.2 us (level); the launches traced: 96.1 us -> 94.7 us
  local copies, waits for them, and re-layouts: 4.23 us -> 2.06 us
  waiting for transfers between devices: 22.3 us -> 23.9 us
    unnamed x12 -> x10, local copies, waits for them, and re-layouts: 3.78 us -> 1.62 us
    all_to_all x1, waiting for transfers between devices: 6.59 us -> 7.55 us  [on_device(): lax.all_to_all(send, 'seq', split_axis=0, concat_axis=0, tiled=True, axis...]
  transfers between devices with their start and end apart: 7 -> 7, of which waited for: 6 -> 6; matrix products, arithmetic and copies ran while one was open for 1% -> 0% of each run, Pallas kernels for 4% -> 4%
where the time goes in v5:
time: 96.2 us; the launch traced here: 94.7 us
  starting transfers between devices  35.3 us (37%)
  waiting for transfers between devices  23.9 us (25%)
  blocking collectives  21.9 us (23%)
  Pallas kernels  8.39 us (9%)
  other arithmetic  2.19 us (2%)
  local copies, waits for them, and re-layouts  2.06 us (2%)
  between operations  0.99 us (1%)
    all_to_all x1, blocking collectives, on_device(): lax.all_to_all(sum_terms(a.reshape(1), part), ('head', 'seq'), split_axis...  21.9 us
    ppermute x3, starting transfers between devices, swap(): lax.ppermute(array, 'tp', [(i, i ^ (flip1 if i % 2 else flip0)) for i in...  17 us
    ppermute x2, starting transfers between devices, on_device(): lax.ppermute(pay, 'seq', [(i, i + k) for i in range(16 - k)])  8.42 us
    all_to_all x1, waiting for transfers between devices, on_device(): lax.all_to_all(send, 'seq', split_axis=0, concat_axis=0, tiled=True, axis...  7.55 us
    all_to_all x1, waiting for transfers between devices, on_device(): lax.all_to_all(dkv, 'seq', split_axis=0, concat_axis=0, tiled=True, axis_...  7.17 us
    ppermute x3, waiting for transfers between devices, swap(): lax.ppermute(array, 'tp', [(i, i ^ (flip1 if i % 2 else flip0)) for i in...  6.98 us
    all_to_all x1, starting transfers between devices, on_device(): lax.all_to_all(dkv, 'seq', split_axis=0, concat_axis=0, tiled=True, axis_...  5.38 us
    all_to_all x1, starting transfers between devices, on_device(): lax.all_to_all(send, 'seq', split_axis=0, concat_axis=0, tiled=True, axis...  4.42 us
  transfers between devices with their start and end apart: 7, of which 6 were waited for; matrix products, arithmetic and copies ran while one was open for 0% of the time, Pallas kernels for 4%

profile of v5, /device:TPU:128, one launch (start us, length us, event | category | flops | bytes accessed | tf_op | source)
XLA Modules:
  0.0 94.7 jit_solution(15512633948320266054)
XLA Ops:
  0.7 0.7 copy-done.3
  1.4 0.8 maximum_bitcast_fusion
  2.5 1.9 %collective-permute-start = (bf16[2,2,24,256]{3,2,0,1:T(8,128)(2,1)S(1)}, bf16[2,2,24,256]{3,2,0,1:T(8,128)(2,1)S(1)}, u32[]{:S(2)}, u32[]{:S(2)}) collective-permute-start(bf16[2,2,24,256]{3,2,0,1:T(8,128)(2,1)S(1)} %get-tuple-element.42), channel_id=1, source_target_pairs={{0,1},{1,0},{2,3},{3,2},{4,5},{5,4},{6,7},{7,6},{8,9},{9,8},{10,11... | collective-permute-start | bytes 147464 | tf_op jit(solution)/shard_map/ppermute | solution.py:296
  4.5 1.2 %collective-permute-done = bf16[2,2,24,256]{3,2,0,1:T(8,128)(2,1)S(1)} collective-permute-done((bf16[2,2,24,256]{3,2,0,1:T(8,128)(2,1)S(1)}, bf16[2,2,24,256]{3,2,0,1:T(8,128)(2,1)S(1)}, u32[]{:S(2)}, u32[]{:S(2)}) %collective-permute-start) | collective-permute-done | bytes 49184 | tf_op jit(solution)/shard_map/ppermute | solution.py:296
  5.7 6.0 %collective-permute-start.1 = (bf16[2,2,24,256]{3,2,1,0:T(8,128)(2,1)S(1)}, bf16[2,2,24,256]{3,2,1,0:T(8,128)(2,1)S(1)}, u32[]{:S(2)}, u32[]{:S(2)}) collective-permute-start(bf16[2,2,24,256]{3,2,1,0:T(8,128)(2,1)S(1)} %get-tuple-element.40), channel_id=1, source_target_pairs={{0,2},{1,7},{2,0},{3,5},{4,6},{5,3},{6,4},{7,1},{8,10},{9,15},{10,... | collective-permute-start | bytes 147464 | tf_op jit(solution)/shard_map/ppermute | solution.py:296
  11.7 3.9 %collective-permute-done.1 = bf16[2,2,24,256]{3,2,1,0:T(8,128)(2,1)S(1)} collective-permute-done((bf16[2,2,24,256]{3,2,1,0:T(8,128)(2,1)S(1)}, bf16[2,2,24,256]{3,2,1,0:T(8,128)(2,1)S(1)}, u32[]{:S(2)}, u32[]{:S(2)}) %collective-permute-start.1) | collective-permute-done | bytes 49184 | tf_op jit(solution)/shard_map/ppermute | solution.py:296
  15.6 9.1 %collective-permute-start.2 = (bf16[2,2,24,256]{3,2,1,0:T(8,128)(2,1)S(1)}, bf16[2,2,24,256]{3,2,1,0:T(8,128)(2,1)S(1)}, u32[]{:S(2)}, u32[]{:S(2)}) collective-permute-start(bf16[2,2,24,256]{3,2,1,0:T(8,128)(2,1)S(1)} %get-tuple-element.38), channel_id=1, source_target_pairs={{0,6},{1,3},{2,4},{3,1},{4,2},{5,7},{6,0},{7,5},{8,14},{9,11},{10,... | collective-permute-start | bytes 147464 | tf_op jit(solution)/shard_map/ppermute | solution.py:296
  24.9 1.9 %collective-permute-done.2 = bf16[2,2,24,256]{3,2,1,0:T(8,128)(2,1)S(1)} collective-permute-done((bf16[2,2,24,256]{3,2,1,0:T(8,128)(2,1)S(1)}, bf16[2,2,24,256]{3,2,1,0:T(8,128)(2,1)S(1)}, u32[]{:S(2)}, u32[]{:S(2)}) %collective-permute-start.2) | collective-permute-done | bytes 49184 | tf_op jit(solution)/shard_map/ppermute | solution.py:296
  27.0 3.0 %collective-permute-start.3 = (bf16[200,256]{1,0:T(8,128)(2,1)S(1)}, bf16[200,256]{1,0:T(8,128)(2,1)S(1)}, u32[]{:S(2)}, u32[]{:S(2)}) collective-permute-start(bf16[200,256]{1,0:T(8,128)(2,1)S(1)} %get-tuple-element.34), channel_id=1, source_target_pairs={{0,32},{8,40},{16,48},{24,56},{32,64},{40,72},{48,80},{56,88},{64,... | collective-permute-start | bytes 307208 | tf_op jit(solution)/shard_map/ppermute | solution.py:310
  30.0 5.4 %collective-permute-start.4 = (bf16[200,256]{1,0:T(8,128)(2,1)S(1)}, bf16[200,256]{1,0:T(8,128)(2,1)S(1)}, u32[]{:S(2)}, u32[]{:S(2)}) collective-permute-start(bf16[200,256]{1,0:T(8,128)(2,1)S(1)} %get-tuple-element.34), channel_id=1, source_target_pairs={{0,64},{8,72},{16,80},{24,88},{32,96},{40,104},{48,112},{56,120},{... | collective-permute-start | bytes 307208 | tf_op jit(solution)/shard_map/ppermute | solution.py:310
  35.5 2.2 %collective-permute-done.4 = bf16[200,256]{1,0:T(8,128)(2,1)S(1)} collective-permute-done((bf16[200,256]{1,0:T(8,128)(2,1)S(1)}, bf16[200,256]{1,0:T(8,128)(2,1)S(1)}, u32[]{:S(2)}, u32[]{:S(2)}) %collective-permute-start.4) | collective-permute-done | bytes 102432 | tf_op jit(solution)/shard_map/ppermute | solution.py:310
  37.8 1.0 %pad_maximum_fusion = bf16[4,2,200,256]{3,2,1,0:T(8,128)(2,1)} fusion(bf16[1,2,200,256]{3,2,1,0:T(8,128)(2,1)S(1)} %broadcast_select_fusion, bf16[1,2,200,256]{3,2,1,0:T(8,128)(2,1)S(1)} %get-tuple-element.31, bf16[1,2,200,256]{3,2,1,0:T(8,128)(2,1)S(1)} %get-tuple-element.30, bf16[1,2,200,256]{3,2,1,0:T(8,128)(2,1)S(1)} %get-tuple-element.29), kind=kLoop, calls=%fused_computation | loop fusion | flops 1228800 | bytes 1638400 | tf_op jit(solution)/shard_map/stack | solution.py:312
  38.8 4.4 %all-to-all-start = ((bf16[4,2,200,256]{3,2,1,0:T(8,128)(2,1)}), bf16[4,2,200,256]{3,2,1,0:T(8,128)(2,1)S(1)}, u32[]{:S(2)}, u32[]{:S(2)}) async-start(bf16[4,2,200,256]{3,2,1,0:T(8,128)(2,1)} %pad_maximum_fusion), calls=%async_computation | async-start | bytes 1638400 | tf_op jit(solution)/shard_map/all_to_all | solution.py:313
  43.3 0.1 broadcast_in_dim_reshape.3.qdoc_ref
  43.5 0.7 copy-done
  44.2 0.1 copy-done.1
  44.3 1.3 %shard_map.85 = (f32[8,1536]{1,0:T(8,128)S(1)}, f32[8,1536]{1,0:T(8,128)S(1)}, f32[1,1536]{1,0:T(1,128)S(1)}) custom-call(s32[1]{0:T(128)} %bitcast.where_ref, s32[1,1536]{1,0:T(1,128)S(1)} %broadcast_in_dim_reshape.3.qdoc_ref, bf16[1536,128]{1,0:T(8,128)(2,1)S(1)} %bitcast.49, bf16[1536,128]{1,0:T(8,128)(2,1)S(1)} %bitcast.52, ...), custom_call_target="tpu_custom_call" | custom-call | flops 536870912 | bytes 5242880 | tf_op jit(solution)/shard_map/pallas_call | solution.py:175
  45.6 7.6 %all-to-all-done.recv_ref = bf16[4,2,200,256]{3,2,1,0:T(8,128)(2,1)S(1)} async-done(((bf16[4,2,200,256]{3,2,1,0:T(8,128)(2,1)}), bf16[4,2,200,256]{3,2,1,0:T(8,128)(2,1)S(1)}, u32[]{:S(2)}, u32[]{:S(2)}) %all-to-all-start) | async-done | bytes 819232 | tf_op jit(solution)/shard_map/all_to_all | solution.py:313
  53.2 3.5 %shard_map.86 = (bf16[4,9,48,256]{3,2,1,0:T(8,128)(2,1)}, f32[1,1536]{1,0:T(1,128)S(1)}) custom-call(s32[1]{0:T(128)} %bitcast.where_ref, s32[1,1536]{1,0:T(1,128)S(1)} %broadcast_in_dim_reshape.3.qdoc_ref, bf16[1536,128]{1,0:T(8,128)(2,1)S(1)} %bitcast.50, bf16[1536,128]{1,0:T(8,128)(2,1)S(1)} %bitcast.53, f32[8,1536]{1,0:T(8,128)S(1)} %get-tuple-element.19.m_ref, ...), custom_call_target="tpu_custom_call" | custom-call | flops 4294967296 | bytes 3145728 | tf_op jit(solution)/shard_map/pallas_call | solution.py:191
  56.6 5.4 %all-to-all-start.1 = ((bf16[4,9,48,256]{3,2,1,0:T(8,128)(2,1)}), bf16[4,9,48,256]{3,2,1,0:T(8,128)(2,1)S(1)}, u32[]{:S(2)}, u32[]{:S(2)}) async-start(bf16[4,9,48,256]{3,2,1,0:T(8,128)(2,1)} %get-tuple-element.23), calls=%async_computation.1 | async-start | bytes 1769472 | tf_op jit(solution)/shard_map/all_to_all | solution.py:320
  62.0 2.8 %shard_map.87 = bf16[1536,128]{1,0:T(8,128)(2,1)} custom-call(s32[1]{0:T(128)} %bitcast.where_ref, s32[1,1536]{1,0:T(1,128)S(1)} %broadcast_in_dim_reshape.3.qdoc_ref, bf16[1536,128]{1,0:T(8,128)(2,1)S(1)} %bitcast.51, bf16[1536,128]{1,0:T(8,128)(2,1)S(1)} %bitcast.54, f32[1,1536]{1,0:T(1,128)S(1)} %get-tuple-element.24.stat_ref, ...), custom_call_target="tpu_custom_call" | custom-call | flops 3221225472 | bytes 3145728 | tf_op jit(solution)/shard_map/pallas_call | solution.py:212
  64.9 7.2 %all-to-all-done.1.part_ref = bf16[4,9,48,256]{3,2,1,0:T(8,128)(2,1)S(1)} async-done(((bf16[4,9,48,256]{3,2,1,0:T(8,128)(2,1)}), bf16[4,9,48,256]{3,2,1,0:T(8,128)(2,1)S(1)}, u32[]{:S(2)}, u32[]{:S(2)}) %all-to-all-start.1) | async-done | bytes 884768 | tf_op jit(solution)/shard_map/all_to_all | solution.py:320
  72.2 21.9 %all_to_all.15.last_ref = bf16[16,48,256]{2,1,0:T(8,128)(2,1)S(1)} all-to-all(bf16[16,48,256]{2,1,0:T(8,128)(2,1)S(1)} %shard_map.88), channel_id=1, replica_groups={{0,32,64,96,128,160,192,224,256,288,320,352,384,416,448,480},{8,40,72,1..., dimensions={0} | all-to-all | bytes 786432 | tf_op jit(solution)/shard_map/all_to_all | solution.py:322
  94.0 0.7 shard_map.89
  (40 shorter events, 0.9 us)
Async XLA Ops:
  0.6 0.8 copy-start.3
  2.5 3.1 %collective-permute-start = (bf16[2,2,24,256]{3,2,0,1:T(8,128)(2,1)S(1)}, bf16[2,2,24,256]{3,2,0,1:T(8,128)(2,1)S(1)}, u32[]{:S(2)}, u32[]{:S(2)}) collective-permute-start(bf16[2,2,24,256]{3,2,0,1:T(8,128)(2,1)S(1)} %get-tuple-element.42), channel_id=1, source_target_pairs={{0,1},{1,0},{2,3},{3,2},{4,5},{5,4},{6,7},{7,6},{8,9},{9,8},{10,11... | collective-permute-start | bytes 147464 | tf_op jit(solution)/shard_map/ppermute | solution.py:296
  5.7 9.9 %collective-permute-start.1 = (bf16[2,2,24,256]{3,2,1,0:T(8,128)(2,1)S(1)}, bf16[2,2,24,256]{3,2,1,0:T(8,128)(2,1)S(1)}, u32[]{:S(2)}, u32[]{:S(2)}) collective-permute-start(bf16[2,2,24,256]{3,2,1,0:T(8,128)(2,1)S(1)} %get-tuple-element.40), channel_id=1, source_target_pairs={{0,2},{1,7},{2,0},{3,5},{4,6},{5,3},{6,4},{7,1},{8,10},{9,15},{10,... | collective-permute-start | bytes 147464 | tf_op jit(solution)/shard_map/ppermute | solution.py:296
  15.6 9.1 %copy-start.4 = (s32[192]{0:T(256)S(1)}, s32[192]{0:T(256)}, u32[]{:S(2)}) copy-start(s32[192]{0:T(256)} %param.9) | copy-start | bytes 2308
  15.6 11.2 %collective-permute-start.2 = (bf16[2,2,24,256]{3,2,1,0:T(8,128)(2,1)S(1)}, bf16[2,2,24,256]{3,2,1,0:T(8,128)(2,1)S(1)}, u32[]{:S(2)}, u32[]{:S(2)}) collective-permute-start(bf16[2,2,24,256]{3,2,1,0:T(8,128)(2,1)S(1)} %get-tuple-element.38), channel_id=1, source_target_pairs={{0,6},{1,3},{2,4},{3,1},{4,2},{5,7},{6,0},{7,5},{8,14},{9,11},{10,... | collective-permute-start | bytes 147464 | tf_op jit(solution)/shard_map/ppermute | solution.py:296
  27.0 8.4 %collective-permute-start.3 = (bf16[200,256]{1,0:T(8,128)(2,1)S(1)}, bf16[200,256]{1,0:T(8,128)(2,1)S(1)}, u32[]{:S(2)}, u32[]{:S(2)}) collective-permute-start(bf16[200,256]{1,0:T(8,128)(2,1)S(1)} %get-tuple-element.34), channel_id=1, source_target_pairs={{0,32},{8,40},{16,48},{24,56},{32,64},{40,72},{48,80},{56,88},{64,... | collective-permute-start | bytes 307208 | tf_op jit(solution)/shard_map/ppermute | solution.py:310
  30.0 7.7 %collective-permute-start.4 = (bf16[200,256]{1,0:T(8,128)(2,1)S(1)}, bf16[200,256]{1,0:T(8,128)(2,1)S(1)}, u32[]{:S(2)}, u32[]{:S(2)}) collective-permute-start(bf16[200,256]{1,0:T(8,128)(2,1)S(1)} %get-tuple-element.34), channel_id=1, source_target_pairs={{0,64},{8,72},{16,80},{24,88},{32,96},{40,104},{48,112},{56,120},{... | collective-permute-start | bytes 307208 | tf_op jit(solution)/shard_map/ppermute | solution.py:310
  38.8 4.7 %copy-start.2 = (bf16[1,192,8,128]{3,2,1,0:T(8,128)(2,1)S(1)}, bf16[1,192,8,128]{3,2,1,0:T(8,128)(2,1)}, u32[]{:S(2)}) copy-start(bf16[1,192,8,128]{3,2,1,0:T(8,128)(2,1)} %param.10) | copy-start | bytes 1179652
  38.8 14.4 %all-to-all-start = ((bf16[4,2,200,256]{3,2,1,0:T(8,128)(2,1)}), bf16[4,2,200,256]{3,2,1,0:T(8,128)(2,1)S(1)}, u32[]{:S(2)}, u32[]{:S(2)}) async-start(bf16[4,2,200,256]{3,2,1,0:T(8,128)(2,1)} %pad_maximum_fusion), calls=%async_computation | async-start | bytes 1638400 | tf_op jit(solution)/shard_map/all_to_all | solution.py:313
  43.2 1.0 %copy-start = (bf16[1,192,8,128]{3,2,1,0:T(8,128)(2,1)S(1)}, bf16[1,192,8,128]{3,2,1,0:T(8,128)(2,1)}, u32[]{:S(2)}) copy-start(bf16[1,192,8,128]{3,2,1,0:T(8,128)(2,1)} %param.11) | copy-start | bytes 1179652
  43.2 1.1 %copy-start.1 = (bf16[1,192,8,128]{3,2,1,0:T(8,128)(2,1)S(1)}, bf16[1,192,8,128]{3,2,1,0:T(8,128)(2,1)}, u32[]{:S(2)}) copy-start(bf16[1,192,8,128]{3,2,1,0:T(8,128)(2,1)} %param.6) | copy-start | bytes 1179652
  56.6 15.4 %all-to-all-start.1 = ((bf16[4,9,48,256]{3,2,1,0:T(8,128)(2,1)}), bf16[4,9,48,256]{3,2,1,0:T(8,128)(2,1)S(1)}, u32[]{:S(2)}, u32[]{:S(2)}) async-start(bf16[4,9,48,256]{3,2,1,0:T(8,128)(2,1)} %get-tuple-element.23), calls=%async_computation.1 | async-start | bytes 1769472 | tf_op jit(solution)/shard_map/all_to_all | solution.py:320
